TPU v7x, 32 devices: a whole 2x2x4 slice. The times are simulated.
32 devices in a mesh: elem: 8 (over z, x), grp: 4 (over y, core).
Axes of the slice: x: 2, y: 2, z: 4, core: 2. Of those that a mesh axis runs over, the one named last changes fastest.
Arguments:
- state: float32 [256, 6, 512], P(('elem', 'grp')), may hold values from -6 to 20, as said below
- material: int32 [256], P(('elem', 'grp')), may hold values from 0 to 1
- metric: float32 [256], P(('elem', 'grp')), may hold values from 1 to 4
- mortar_proj: float32 [4, 64, 64], replicated, may hold values from 0 to 1, as said below
- mortar_map: int32 [32, 4, 96], P(('elem', 'grp')), may hold values from 0 to 7, as said below
- mortar_count: int32 [32, 6], P(('elem', 'grp')), may hold values from 0 to 32, as said below
- neighbours: int32 [256, 6], P(('elem', 'grp')), may hold values from -1 to 7, as said below
Outputs:
- new_state: float32 [256, 6, 512], P(('elem', 'grp'))
Inputs may be any that keep to these rules, and one draw needn't show every extreme that they name: `state`: density and pressure, with either heat ratio, are positive at every node. `mortar_proj`: entries are nonnegative and every row sums to one. `mortar_map`: Rows: local element, face (0 to 5), subface (0 conforming, 1 to 4 a quadrant of a coarse face), orientation (0 to 7). Slot s below 32 pairs with slot (own grp index) * 8 + s % 8 of the device with the same elem index and grp index s // 8; the next 32 slots pair, position by position, with the last 32 slots of the device one elem index higher, the last 32 with the middle 32 of the device one elem index lower, same grp index. Paired faces lie along one dimension with opposite normals; at most one side of a pair has a nonzero subface. `mortar_count`: entry g below 4 counts the live slots toward grp peer g, 0 for the device itself, equal to the peer's entry for this device, at most 8 and reaching it on some devices; entry 4 toward the next elem index equals that device's entry 5; the top elem index has 0 in entry 4, the bottom one 0 in entry 5. Slots at positions below the count are live. `neighbours`: local element across the face, meeting its opposite face, or -1.
All inputs are finite; a program needn't handle non-finite values.
Results may differ from a plain program's by a relative error of at most 0.0003.
Values sent between devices are 32-bit elements; how exact they have to be, the bound alone decides.
A program may use at most 64 MiB of HBM per device.

v0:
```python
import jax
import jax.numpy as jnp
import numpy as np
from jax import lax
from jax.sharding import PartitionSpec as P

NV = 6
NP = 8
FN = 64
VN = 512
SUBS = 4
CAPG = 8
CAPS = 32


highest = lax.Precision.HIGHEST
step_size = 0.002
lift_weight = 49.0


def from_behind(block, axis, distance):
    devices = range(lax.axis_size(axis))
    route = [(i - distance, i) for i in devices if i - distance in devices]
    return lax.ppermute(block, axis, route)


def cheb_matrix():
    points = -np.cos(np.pi * np.arange(8) / 7.0)
    factor = np.array([2.0, 1.0, 1.0, 1.0, 1.0, 1.0, 1.0, 2.0])
    alternating = np.where(np.arange(8) % 2 == 0, 1.0, -1.0)
    scaled = factor * alternating
    differ = points[:, None] - points[None, :] + np.eye(8)
    matrix = scaled[:, None] / scaled[None, :] / differ
    matrix = matrix * (1.0 - np.eye(8))
    return matrix - np.eye(8) * matrix.sum(axis=1)[:, None]


def face_plane(node_grid, face):
    index = 0 if face % 2 == 0 else 7
    if face // 2 == 0:
        return node_grid[index]
    if face // 2 == 1:
        return node_grid[:, index]
    return node_grid[:, :, index]


def face_select():
    node_grid = np.arange(512).reshape(8, 8, 8)
    layers = []
    for face in range(6):
        layers.append(face_plane(node_grid, face).reshape(64))
    nodes = np.concatenate(layers)
    return (nodes[:, None] == np.arange(512)[None, :]).astype(np.float32)


def orient_matrices():
    first, second = np.meshgrid(np.arange(8), np.arange(8), indexing="ij")
    result = []
    for orient in range(8):
        row_p, row_r = (second, first) if orient & 4 else (first, second)
        if orient & 1:
            row_p = 7 - row_p
        if orient & 2:
            row_r = 7 - row_r
        source = (8 * row_p + row_r).reshape(64)
        result.append((source[:, None] == np.arange(64)[None, :]).astype(np.float32))
    return np.stack(result)


def state_parts(cons, heat_ratio, normal):
    density = cons[:, 0]
    momentum = cons[:, 1:4]
    energy = cons[:, 4]
    scalar = cons[:, 5]
    velocity = momentum / density[:, None]
    pressure = (heat_ratio[:, None] - 1.0) * (energy - 0.5 * jnp.sum(momentum * velocity, axis=1))
    direction = normal[:, :, None]
    speed_n = jnp.sum(direction * velocity, axis=1)
    sound_speed = jnp.sqrt(heat_ratio[:, None] * pressure / density)
    phys_flux = jnp.concatenate(
        [
            (density * speed_n)[:, None],
            momentum * speed_n[:, None] + pressure[:, None] * direction,
            ((energy + pressure) * speed_n)[:, None],
            (scalar * speed_n)[:, None],
        ],
        axis=1,
    )
    return (density, velocity, pressure, speed_n, sound_speed, energy, scalar, phys_flux)


def star_state(parts, wave_speed, middle, normal):
    density, velocity, pressure, speed_n, sound_speed, energy, scalar, phys_flux = parts
    relative = wave_speed - speed_n
    factor = density * relative / (wave_speed - middle)
    shifted = middle - speed_n
    momentum = factor[:, None] * (velocity + shifted[:, None] * normal[:, :, None])
    energy_star = factor * (energy / density + shifted * (middle + pressure / (density * relative)))
    return jnp.concatenate(
        [factor[:, None], momentum, energy_star[:, None], (factor * scalar / density)[:, None]],
        axis=1,
    )


def hllc_flux(left, right, heat_left, heat_right, normal):
    left_parts = state_parts(left, heat_left, normal)
    right_parts = state_parts(right, heat_right, normal)
    left_wave = jnp.minimum(left_parts[3] - left_parts[4], right_parts[3] - right_parts[4])
    right_wave = jnp.maximum(left_parts[3] + left_parts[4], right_parts[3] + right_parts[4])
    left_mass = left_parts[0] * (left_wave - left_parts[3])
    right_mass = right_parts[0] * (right_wave - right_parts[3])
    middle = (
        right_parts[2] - left_parts[2] + left_mass * left_parts[3] - right_mass * right_parts[3]
    ) / (left_mass - right_mass)
    left_star = left_parts[7] + left_wave[:, None] * (
        star_state(left_parts, left_wave, middle, normal) - left
    )
    right_star = right_parts[7] + right_wave[:, None] * (
        star_state(right_parts, right_wave, middle, normal) - right
    )
    return jnp.where(
        (left_wave >= 0.0)[:, None],
        left_parts[7],
        jnp.where(
            (middle >= 0.0)[:, None],
            left_star,
            jnp.where((right_wave > 0.0)[:, None], right_star, right_parts[7]),
        ),
    )


def normals_of(face):
    axis_id = face // 2
    orient_sign = jnp.where(face % 2 == 1, 1.0, -1.0).astype(jnp.float32)
    return orient_sign[:, None] * (
        axis_id[:, None] == jnp.arange(3, dtype=jnp.int32)[None, :]
    ).astype(jnp.float32)


def face_traces(elements, select):
    count_el = elements.shape[0]
    flat_state = elements.reshape(count_el * NV, VN)
    traces = jnp.dot(flat_state, select.T, precision=highest, preferred_element_type=jnp.float32)
    return traces.reshape(count_el, NV, 6, FN).transpose(0, 2, 1, 3).reshape(count_el * 6, NV, FN)


def slot_operators(mortar_proj, mortar_info):
    identity = jnp.eye(FN, dtype=jnp.float32)
    proj_table = jnp.concatenate([identity[None], mortar_proj], axis=0)
    orients = jnp.asarray(orient_matrices(), jnp.float32)
    combos = jnp.einsum("spq,oqr->sopr", proj_table, orients, precision=highest).reshape(
        (SUBS + 1) * 8, FN, FN
    )
    return combos[mortar_info[2] * 8 + mortar_info[3]]


def mortar_traces(face_rows, operators, heat_ratio, mortar_info):
    picked = face_rows[mortar_info[0] * 6 + mortar_info[1]]
    native = jnp.einsum("spq,svq->svp", operators, picked, precision=highest)
    return (native, heat_ratio[mortar_info[0]])


def slot_layout(groups, grp_index, counts):
    grp_slots = groups * CAPG
    slot_index = jnp.arange(grp_slots + 2 * CAPS, dtype=jnp.int32)
    peer_index = slot_index // CAPG
    in_grp = slot_index < grp_slots
    in_up = (slot_index >= grp_slots) & (slot_index < grp_slots + CAPS)
    group_id = jnp.where(in_grp, peer_index, jnp.where(in_up, groups, groups + 1))
    position = jnp.where(in_grp, slot_index % CAPG, (slot_index - grp_slots) % CAPS)
    slot_limit = jnp.sum(
        jnp.where(
            group_id[:, None] == jnp.arange(groups + 2, dtype=jnp.int32)[None, :],
            counts[None, :],
            0,
        ),
        axis=1,
    )
    is_live = position < slot_limit
    is_lower = jnp.where(in_grp, grp_index < peer_index, in_up)
    return (is_lower, is_live)


def mortar_flux(native, partner, native_heat, partner_heat, normal, is_lower, is_live):
    live_mask = is_live[:, None, None]
    partner = jnp.where(live_mask, partner, native)
    partner_heat = jnp.where(is_live, partner_heat, native_heat)
    lower_mask = is_lower[:, None, None]
    low_side = jnp.where(lower_mask, native, partner)
    high_side = jnp.where(lower_mask, partner, native)
    low_heat = jnp.where(is_lower, native_heat, partner_heat)
    high_heat = jnp.where(is_lower, partner_heat, native_heat)
    low_normal = jnp.where(is_lower[:, None], normal, -normal)
    return hllc_flux(low_side, high_side, low_heat, high_heat, low_normal)


def volume_term(elements, heat_ratio):
    count_el = elements.shape[0]
    deriv = jnp.asarray(cheb_matrix(), jnp.float32)
    fluxes = []
    for axis_id in range(3):
        direction = jnp.eye(3, dtype=jnp.float32)[axis_id][None, :]
        fluxes.append(
            state_parts(elements, heat_ratio, direction)[7].reshape(count_el, NV, NP, NP, NP)
        )
    total = jnp.einsum("ia,evabc->evibc", deriv, fluxes[0], precision=highest)
    total = total + jnp.einsum("jb,evabc->evajc", deriv, fluxes[1], precision=highest)
    total = total + jnp.einsum("kc,evabc->evabk", deriv, fluxes[2], precision=highest)
    return -total.reshape(count_el, NV, VN)


def section_update(
    elements,
    heat_ratio,
    metric,
    mortar_info,
    neighbours,
    face_rows,
    operators,
    native,
    native_heat,
    flux_own,
    is_live,
    select,
    volume,
):
    count_el = elements.shape[0]
    normal = normals_of(mortar_info[1])
    correction = state_parts(native, native_heat, normal)[7] - flux_own
    correction = jnp.where(is_live[:, None, None], correction, 0.0)
    back_weight = jnp.where(mortar_info[2] == 0, 1.0, 0.25).astype(jnp.float32)
    projected = back_weight[:, None, None] * jnp.einsum(
        "spq,svp->svq", operators, correction, precision=highest
    )
    face_id = jnp.tile(jnp.arange(6, dtype=jnp.int32), count_el)
    face_owner = jnp.repeat(jnp.arange(count_el, dtype=jnp.int32), 6)
    face_normal = normals_of(face_id)
    across = neighbours.reshape(count_el * 6)
    has_across = across >= 0
    safe_across = jnp.where(has_across, across, face_owner)
    source = jnp.where(
        has_across,
        across * 6 + jnp.bitwise_xor(face_id, 1),
        jnp.arange(count_el * 6, dtype=jnp.int32),
    )
    partner = face_rows[source]
    row_heat = heat_ratio[face_owner]
    local_term = state_parts(face_rows, row_heat, face_normal)[7] - hllc_flux(
        face_rows, partner, row_heat, heat_ratio[safe_across], face_normal
    )
    local_term = jnp.where(has_across[:, None, None], local_term, 0.0)
    face_sum = local_term + jax.ops.segment_sum(
        projected, mortar_info[0] * 6 + mortar_info[1], num_segments=count_el * 6
    )
    placed = (
        face_sum.reshape(count_el, 6, NV, FN).transpose(0, 2, 1, 3).reshape(count_el * NV, 6 * FN)
    )
    surface = jnp.dot(
        placed, select, precision=highest, preferred_element_type=jnp.float32
    ).reshape(count_el, NV, VN)
    return elements + step_size * metric[:, None, None] * (volume + lift_weight * surface)


def shards(state, material, metric, mortar_proj, mortar_map, mortar_count, neighbours):
    select = jnp.asarray(face_select(), jnp.float32)
    mortar_info = mortar_map[0]
    counts = mortar_count[0]
    groups = lax.axis_size("grp")
    grp_index = lax.axis_index("grp")
    heat_ratio = 1.4 + 0.27 * material.astype(jnp.float32)
    face_rows = face_traces(state, select)
    operators = slot_operators(mortar_proj, mortar_info)
    native, native_heat = mortar_traces(face_rows, operators, heat_ratio, mortar_info)
    is_lower, is_live = slot_layout(groups, grp_index, counts)
    normal = normals_of(mortar_info[1])
    grp_slots = groups * CAPG
    upper_end = grp_slots + CAPS
    row_width = NV * FN
    arrived, arrived_heat = (
        lax.all_to_all(
            native[:grp_slots].reshape(groups, CAPG, row_width),
            "grp",
            split_axis=0,
            concat_axis=0,
            tiled=True,
        ),
        lax.all_to_all(
            native_heat[:grp_slots].reshape(groups, CAPG),
            "grp",
            split_axis=0,
            concat_axis=0,
            tiled=True,
        ),
    )
    arrived = arrived.reshape(grp_slots, NV, FN)
    arrived_heat = arrived_heat.reshape(grp_slots)
    from_below, below_heat = from_behind(
        (native[grp_slots:upper_end].reshape(CAPS, row_width), native_heat[grp_slots:upper_end]),
        "elem",
        1,
    )
    from_below = from_below.reshape(CAPS, NV, FN)
    from_above, above_heat = from_behind(
        (native[upper_end:].reshape(CAPS, row_width), native_heat[upper_end:]), "elem", -1
    )
    partner = jnp.concatenate([arrived, from_above.reshape(CAPS, NV, FN), from_below], axis=0)
    partner_heat = jnp.concatenate([arrived_heat, above_heat, below_heat], axis=0)
    star_flux = mortar_flux(native, partner, native_heat, partner_heat, normal, is_lower, is_live)
    flux_own = jnp.where(is_lower[:, None, None], star_flux, -star_flux)
    volume = volume_term(state, heat_ratio)
    return section_update(
        state,
        heat_ratio,
        metric,
        mortar_info,
        neighbours,
        face_rows,
        operators,
        native,
        native_heat,
        flux_own,
        is_live,
        select,
        volume,
    )


def solution(mesh):
    return jax.shard_map(
        shards,
        mesh=mesh,
        in_specs=(
            P(("elem", "grp"), None, None),
            P(("elem", "grp")),
            P(("elem", "grp")),
            P(),
            P(("elem", "grp"), None, None),
            P(("elem", "grp"), None),
            P(("elem", "grp"), None),
        ),
        out_specs=P(("elem", "grp"), None, None),
        check_vma=False,
    )
```

profile of v0, /device:TPU:0, one launch (start us, length us, event | category | flops | bytes accessed | tf_op | source)
XLA Modules:
  0.0 189.8 jit_solution(14438648100474914285)
XLA Ops:
  1.9 6.2 %broadcast_add_fusion.2 = (f32[96]{0:T(128)}, f32[96]{0:T(128)S(1)}) fusion(f32[]{:T(128)} %bitcast.29, f32[]{:T(128)} %bitcast.28, f32[]{:T(128)} %bitcast.27, f32[]{:T(128)} %bitcast.26, f32[]{:T(128)} %bitcast.25, f32[]{:T(128)} %bitcast.24, f32[]{:T(128)} %bitcast.23, f32[]{:T(128)} %bitcast.22, s32[1,4,96]{2,1,0:T(4,128)} %param.14), kind=kLoop, calls=%fused_computation.290 | loop fusion | flops 1728 | bytes 1184 | tf_op jit(solution)/shard_map/sub | solution.py:76
  8.7 5.4 %collective-permute-start.3 = (f32[32]{0:T(128)}, f32[32]{0:T(128)}, u32[]{:S(2)}, u32[]{:S(2)}) collective-permute-start(f32[32]{0:T(128)} %get-tuple-element.138), channel_id=1, source_target_pairs={{0,4},{4,8},{8,12},{12,16},{16,20},{20,24},{24,28},{1,5},{5,9},{9,... | collective-permute-start | bytes 392 | tf_op jit(solution)/shard_map/ppermute | solution.py:24
  16.0 3.7 %all-to-all-start.1 = ((f32[4,1,8]{2,1,0:T(1,128)}), f32[4,1,8]{2,1,0:T(1,128)}, u32[]{:S(2)}, u32[]{:S(2)}) async-start(f32[4,1,8]{2,1,0:T(1,128)} %bitcast.84), calls=%async_computation.1 | async-start | bytes 4096 | tf_op jit(solution)/shard_map/all_to_all | solution.py:287
  21.2 2.3 %convolution_bitcast_fusion = f32[8,6,6,64]{3,0,2,1:T(8,128)S(1)} fusion(f32[6,64,512,1]{2,1,3,0:T(8,128)} %constant.204, f32[8,6,512]{2,0,1:T(8,128)} %param.10), kind=kOutput, calls=%fused_computation.27 | convolution fusion | flops 113246208 | bytes 958464 | tf_op jit(solution)/shard_map/dot_general | solution.py:143
  25.2 2.3 %fusion.37 = f32[5,64,8,64]{3,1,2,0:T(8,128)} fusion(f32[8,64,64,1]{2,1,0,3:T(8,128)S(1)} %copy-done.21, f32[4,64,64]{2,1,0:T(8,128)S(1)} %copy-done.30, f32[1,64,64]{2,1,0:T(8,128)S(1)} %fusion.51), kind=kOutput, calls=%fused_computation.59 | convolution fusion | flops 125849600 | bytes 868352 | tf_op jit(solution)/shard_map/spq,oqr->sopr/dot_general | solution.py:151
  27.5 2.1 %gather_fusion.2 = f32[96,64,64]{2,1,0:T(8,128)S(1)} fusion(f32[40,64,64]{2,1,0:T(8,128)} %bitcast.399, s32[1024]{0:T(1024)S(1)} %get-tuple-element.152), kind=kCustom, calls=%fused_computation.2 | custom fusion | bytes 3146112 | tf_op jit(solution)/shard_map/gather | solution.py:154
  29.5 6.0 %fusion.106 = f32[96,6,64]{2,1,0:T(8,128)S(1)} fusion(f32[96,6,64]{2,1,0:T(8,128)} %gather_fusion.1, f32[96,64,64]{2,1,0:T(8,128)S(1)} %gather_fusion.2), kind=kOutput, calls=%fused_computation.304 | convolution fusion | flops 28311552 | bytes 1867776 | tf_op jit(solution)/shard_map/spq,svq->svp/dot_general | solution.py:159
  38.6 5.2 %collective-permute-start.1 = (f32[32,384]{1,0:T(8,128)}, f32[32,384]{1,0:T(8,128)}, u32[]{:S(2)}, u32[]{:S(2)}) collective-permute-start(f32[32,384]{1,0:T(8,128)} %reshape.1613), channel_id=1, source_target_pairs={{0,4},{4,8},{8,12},{12,16},{16,20},{20,24},{24,28},{1,5},{5,9},{9,... | collective-permute-start | bytes 147464 | tf_op jit(solution)/shard_map/ppermute | solution.py:24
  51.2 1.8 copy.212
  58.6 1.8 copy.187
  63.3 1.8 copy.186
  66.6 2.2 %concatenate.94 = f32[8,3,8,8,8]{4,3,2,0,1:T(8,128)} reshape(f32[8,3,512]{2,0,1:T(8,128)} %get-tuple-element.93) | data formatting | bytes 98304 | tf_op jit(solution)/shard_map/concatenate | solution.py:80
  68.8 2.3 %copy.185 = f32[8,3,8,8,8]{3,4,2,1,0:T(8,128)} copy(f32[8,3,8,8,8]{4,3,2,0,1:T(8,128)} %concatenate.94) | data formatting | bytes 98304 | tf_op jit(solution)/shard_map/concatenate | solution.py:80
  72.0 1.8 copy.184
  73.8 3.9 %fusion.8 = f32[8,6,8,8,8]{4,3,2,1,0:T(8,128)} fusion(f32[8,8,1,1,1]{1,0,4,3,2:T(8,128)S(1)} %copy-done.32, f32[8,1,8,8,8]{3,4,2,1,0:T(8,128)} %copy.187, f32[8,1,8,8,8]{3,4,2,1,0:T(8,128)} %copy.186, f32[8,3,8,8,8]{3,4,2,1,0:T(8,128)} %copy.185, f32[8,1,8,8,8]{3,4,2,1,0:T(8,128)} %copy.184), kind=kOutput, calls=%fused_computation.12 | convolution fusion | flops 2433024 | bytes 196864 | tf_op jit(solution)/shard_map/jb,evabc->evajc/dot_general | solution.py:207
  77.6 3.1 %copy.188 = f32[8,6,8,8,8]{2,3,4,1,0:T(8,128)} copy(f32[8,6,8,8,8]{4,3,2,1,0:T(8,128)} %fusion.8) | data formatting | bytes 196608 | tf_op jit(solution)/shard_map/jb,evabc->evajc/dot_general | solution.py:207
  82.3 1.8 copy.183
  85.7 1.8 copy.182
  88.8 2.3 %copy.181 = f32[8,3,8,8,8]{2,4,3,1,0:T(8,128)} copy(f32[8,3,8,8,8]{4,3,2,0,1:T(8,128)} %concatenate.89) | data formatting | bytes 98304 | tf_op jit(solution)/shard_map/concatenate | solution.py:80
  91.1 1.6 concatenate.88
  92.7 1.8 copy.180
  99.9 2.9 %fusion = f32[8,6,8,8,8]{4,3,2,1,0:T(8,128)S(1)} fusion(f32[8,8,1,1,1]{1,0,4,3,2:T(8,128)} %constant.203, f32[8,1,8,8,8]{2,4,3,1,0:T(8,128)} %copy.183, f32[8,1,8,8,8]{2,4,3,1,0:T(8,128)} %copy.182, f32[8,3,8,8,8]{2,4,3,1,0:T(8,128)} %copy.181, f32[8,1,8,8,8]{2,4,3,1,0:T(8,128)} %copy.180), kind=kOutput, calls=%fused_computation.4 | convolution fusion | flops 2433024 | bytes 196864 | tf_op jit(solution)/shard_map/ia,evabc->evibc/dot_general | solution.py:206
  104.3 22.2 %fusion.17 = f32[8,6,8,8,8]{2,4,3,1,0:T(8,128)} fusion(f32[8,6,8,8,8]{2,3,4,1,0:T(8,128)S(1)} %copy-done, f32[8,6,8,8,8]{4,3,2,1,0:T(8,128)S(1)} %fusion, f32[8,8,1,1,1]{1,0,4,3,2:T(8,128)S(1)} %copy-done.33, f32[8,6,8,8,8]{4,3,2,1,0:T(8,128)S(1)} %pad_maximum_fusion), kind=kOutput, calls=%fused_computation.23 | convolution fusion | flops 2433024 | bytes 393472 | tf_op jit(solution)/shard_map/kc,evabc->evabk/dot_general | solution.py:208
  126.5 3.0 %copy.191 = f32[8,6,8,8,8]{4,3,2,0,1:T(8,128)} copy(f32[8,6,8,8,8]{2,4,3,1,0:T(8,128)} %fusion.17) | data formatting | bytes 196608 | tf_op jit(solution)/shard_map/neg | solution.py:209
  129.5 2.9 %neg.17 = f32[8,6,512]{2,0,1:T(8,128)} reshape(f32[8,6,8,8,8]{4,3,2,0,1:T(8,128)} %copy.191) | data formatting | bytes 196608 | tf_op jit(solution)/shard_map/neg | solution.py:209
  133.8 1.8 fusion.103
  135.7 5.6 %broadcast_add_fusion.4 = (f32[48]{0:T(128)}, f32[48]{0:T(128)S(1)}, f32[48]{0:T(128)}, f32[48]{0:T(128)S(1)}) fusion(f32[]{:T(128)} %bitcast.29, f32[]{:T(128)} %bitcast.28, f32[]{:T(128)} %bitcast.27, f32[]{:T(128)} %bitcast.26, f32[]{:T(128)} %bitcast.25, f32[]{:T(128)} %bitcast.24, f32[]{:T(128)} %bitcast.23, f32[]{:T(128)} %bitcast.22, ...), kind=kLoop, calls=%fused_computation.292 | loop fusion | flops 1824 | bytes 1184 | tf_op jit(solution)/shard_map/sub | solution.py:76
  160.2 3.5 %all-to-all-start = ((f32[4,8,384]{2,1,0:T(8,128)}), f32[4,8,384]{2,1,0:T(8,128)S(1)}, u32[]{:S(2)}, u32[]{:S(2)}) async-start(f32[4,8,384]{2,1,0:T(8,128)} %reshape.1609), calls=%async_computation | async-start | bytes 98304 | tf_op jit(solution)/shard_map/all_to_all | solution.py:280
  169.9 1.6 copy.231
  171.6 1.6 copy.230
  176.5 4.5 %convolution_multiply_fusion = f32[96,6,64]{2,1,0:T(8,128)} fusion(f32[96,6,64]{2,1,0:T(8,128)} %copy.223, f32[96,64,64]{2,1,0:T(8,128)S(1)} %gather_fusion.2, f32[96]{0:T(128)S(1)} %copy-done.50), kind=kOutput, calls=%fused_computation.26 | convolution fusion | flops 28348416 | bytes 1868160 | tf_op jit(solution)/shard_map/spq,svp->svq/dot_general | solution.py:232
  181.0 7.3 %scatter_fusion = f32[48,6,64]{2,1,0:T(8,128)S(1)} fusion(f32[48,6,64]{2,1,0:T(8,128)S(1)} %fusion.26, s32[96]{0:T(128)S(1)} %bitcast.438, f32[96,6,64]{2,1,0:T(8,128)} %convolution_multiply_fusion), kind=kCustom, calls=%fused_computation.3 | custom fusion | flops 36864 | bytes 442752 | tf_op jit(solution)/shard_map/scatter-add | solution.py:252
  (210 shorter events, 71.1 us)
Async XLA Ops:
  0.0 25.2 %copy-start.21 = (f32[8,64,64,1]{2,1,0,3:T(8,128)S(1)}, f32[8,64,64,1]{2,1,0,3:T(8,128)}, u32[]{:S(2)}) copy-start(f32[8,64,64,1]{2,1,0,3:T(8,128)} %constant.205) | copy-start | bytes 393220
  0.0 25.2 %copy-start.30 = (f32[4,64,64]{2,1,0:T(8,128)S(1)}, f32[4,64,64]{2,1,0:T(8,128)}, u32[]{:S(2)}) copy-start(f32[4,64,64]{2,1,0:T(8,128)} %param.13) | copy-start | bytes 196612
  8.1 11.6 %copy-start.36 = (f32[96]{0:T(128)}, f32[96]{0:T(128)S(1)}, u32[]{:S(2)}) copy-start(f32[96]{0:T(128)S(1)} %get-tuple-element.37) | copy-start | bytes 1156
  8.7 157.0 %collective-permute-start.3 = (f32[32]{0:T(128)}, f32[32]{0:T(128)}, u32[]{:S(2)}, u32[]{:S(2)}) collective-permute-start(f32[32]{0:T(128)} %get-tuple-element.138), channel_id=1, source_target_pairs={{0,4},{4,8},{8,12},{12,16},{16,20},{20,24},{24,28},{1,5},{5,9},{9,... | collective-permute-start | bytes 392 | tf_op jit(solution)/shard_map/ppermute | solution.py:24
  14.1 151.6 %collective-permute-start.2 = (f32[32]{0:T(128)}, f32[32]{0:T(128)}, u32[]{:S(2)}, u32[]{:S(2)}) collective-permute-start(f32[32]{0:T(128)} %get-tuple-element.139), channel_id=1, source_target_pairs={{4,0},{8,4},{12,8},{16,12},{20,16},{24,20},{28,24},{5,1},{9,5},{13... | collective-permute-start | bytes 392 | tf_op jit(solution)/shard_map/ppermute | solution.py:24
  16.0 144.2 %all-to-all-start.1 = ((f32[4,1,8]{2,1,0:T(1,128)}), f32[4,1,8]{2,1,0:T(1,128)}, u32[]{:S(2)}, u32[]{:S(2)}) async-start(f32[4,1,8]{2,1,0:T(1,128)} %bitcast.84), calls=%async_computation.1 | async-start | bytes 4096 | tf_op jit(solution)/shard_map/all_to_all | solution.py:287
  29.5 20.5 %copy-start.37 = (s32[8,6]{1,0:T(8,128)S(1)}, s32[8,6]{1,0:T(8,128)}, u32[]{:S(2)}) copy-start(s32[8,6]{1,0:T(8,128)} %param.16) | copy-start | bytes 580
  36.3 16.7 %copy-start.44 = (s32[1,4,96]{2,1,0:T(4,128)S(1)}, s32[1,4,96]{2,1,0:T(4,128)}, u32[]{:S(2)}) copy-start(s32[1,4,96]{2,1,0:T(4,128)} %param.14) | copy-start | bytes 4612
  38.6 131.3 %collective-permute-start.1 = (f32[32,384]{1,0:T(8,128)}, f32[32,384]{1,0:T(8,128)}, u32[]{:S(2)}, u32[]{:S(2)}) collective-permute-start(f32[32,384]{1,0:T(8,128)} %reshape.1613), channel_id=1, source_target_pairs={{0,4},{4,8},{8,12},{12,16},{16,20},{20,24},{24,28},{1,5},{5,9},{9,... | collective-permute-start | bytes 147464 | tf_op jit(solution)/shard_map/ppermute | solution.py:24
  45.4 126.2 %collective-permute-start = (f32[32,384]{1,0:T(8,128)}, f32[32,384]{1,0:T(8,128)}, u32[]{:S(2)}, u32[]{:S(2)}) collective-permute-start(f32[32,384]{1,0:T(8,128)} %reshape.1611), channel_id=1, source_target_pairs={{4,0},{8,4},{12,8},{16,12},{20,16},{24,20},{28,24},{5,1},{9,5},{13... | collective-permute-start | bytes 147464 | tf_op jit(solution)/shard_map/ppermute | solution.py:24
  66.6 7.1 %copy-start.32 = (f32[8,8,1,1,1]{1,0,4,3,2:T(8,128)S(1)}, f32[8,8,1,1,1]{1,0,4,3,2:T(8,128)}, u32[]{:S(2)}) copy-start(f32[8,8,1,1,1]{1,0,4,3,2:T(8,128)} %constant.203) | copy-start | bytes 772
  88.8 9.7 %copy-start.25 = (f32[8,3,512]{2,0,1:T(8,128)S(1)}, f32[8,3,512]{2,0,1:T(8,128)}, u32[]{:S(2)}) copy-start(f32[8,3,512]{2,0,1:T(8,128)} %get-tuple-element.91) | copy-start | bytes 147460
  129.5 11.8 %copy-start.49 = (pred[8,6]{1,0:T(8,128)(4,1)S(1)}, pred[8,6]{1,0:T(8,128)(4,1)}, u32[]{:S(2)}) copy-start(pred[8,6]{1,0:T(8,128)(4,1)} %broadcast_compare_fusion) | copy-start | bytes 148
  129.5 12.5 %copy-start.52 = (f32[48]{0:T(128)S(1)}, f32[48]{0:T(128)}, u32[]{:S(2)}) copy-start(f32[48]{0:T(128)} %compare_select_fusion.31) | copy-start | bytes 580
  129.5 12.5 %copy-start.53 = (s32[48]{0:T(128)S(1)}, s32[48]{0:T(128)}, u32[]{:S(2)}) copy-start(s32[48]{0:T(128)} %and_select_fusion.6) | copy-start | bytes 580
  147.0 10.1 %copy-start.3 = (f32[48,6,64]{2,1,0:T(8,128)S(1)}, f32[48,6,64]{2,1,0:T(8,128)}, u32[]{:S(2)}) copy-start(f32[48,6,64]{2,1,0:T(8,128)} %gather_fusion) | copy-start | bytes 221188
  147.0 10.1 %copy-start.10 = (f32[48,64]{1,0:T(8,128)S(1)}, f32[48,64]{1,0:T(8,128)}, u32[]{:S(2)}) copy-start(f32[48,64]{1,0:T(8,128)} %copy-done.9) | copy-start | bytes 36868
  147.0 10.1 %copy-start.15 = (f32[48,1,64]{2,0,1:T(8,128)S(1)}, f32[48,1,64]{2,0,1:T(8,128)}, u32[]{:S(2)}) copy-start(f32[48,1,64]{2,0,1:T(8,128)} %copy-done.14) | copy-start | bytes 36868
  147.0 10.1 %copy-start.17 = (f32[48,1,64]{2,0,1:T(8,128)S(1)}, f32[48,1,64]{2,0,1:T(8,128)}, u32[]{:S(2)}) copy-start(f32[48,1,64]{2,0,1:T(8,128)} %copy-done.16) | copy-start | bytes 36868
  147.0 10.1 %copy-start.22 = (f32[48,64]{1,0:T(8,128)S(1)}, f32[48,64]{1,0:T(8,128)}, u32[]{:S(2)}) copy-start(f32[48,64]{1,0:T(8,128)} %slice_bitcast_fusion.3) | copy-start | bytes 36868
  147.0 10.1 %copy-start.24 = (f32[48,3]{1,0:T(8,128)S(1)}, f32[48,3]{1,0:T(8,128)}, u32[]{:S(2)}) copy-start(f32[48,3]{1,0:T(8,128)} %copy-done.23) | copy-start | bytes 1732
  147.0 10.4 %copy-start.13 = (f32[48,1,64]{2,0,1:T(8,128)S(1)}, f32[48,1,64]{2,0,1:T(8,128)}, u32[]{:S(2)}) copy-start(f32[48,1,64]{2,0,1:T(8,128)} %copy-done.12) | copy-start | bytes 36868
  147.0 10.4 %copy-start.20 = (f32[48,1,64]{2,0,1:T(8,128)S(1)}, f32[48,1,64]{2,0,1:T(8,128)}, u32[]{:S(2)}) copy-start(f32[48,1,64]{2,0,1:T(8,128)} %copy-done.19) | copy-start | bytes 36868
  147.0 10.4 %copy-start.34 = (pred[48,64]{1,0:T(8,128)(4,1)S(1)}, pred[48,64]{1,0:T(8,128)(4,1)}, u32[]{:S(2)}) copy-start(pred[48,64]{1,0:T(8,128)(4,1)} %get-tuple-element.46) | copy-start | bytes 9220
  147.0 7.1 %copy-start.42 = (pred[96]{0:T(512)(128)(4,1)}, pred[96]{0:T(512)(128)(4,1)S(1)}, u32[]{:S(2)}) copy-start(pred[96]{0:T(512)(128)(4,1)S(1)} %compare_select_fusion.28) | copy-start | bytes 292
  157.3 8.4 %copy-start.54 = (s32[96]{0:T(128)S(1)}, s32[96]{0:T(128)}, u32[]{:S(2)}) copy-start(s32[96]{0:T(128)} %select_reduce_fusion) | copy-start | bytes 1156
  158.6 15.9 %copy-start.35 = (f32[96,3]{0,1:T(4,128)S(1)}, f32[96,3]{0,1:T(4,128)}, u32[]{:S(2)}) copy-start(f32[96,3]{0,1:T(4,128)} %get-tuple-element.135) | copy-start | bytes 3460
  160.2 7.9 %all-to-all-start = ((f32[4,8,384]{2,1,0:T(8,128)}), f32[4,8,384]{2,1,0:T(8,128)S(1)}, u32[]{:S(2)}, u32[]{:S(2)}) async-start(f32[4,8,384]{2,1,0:T(8,128)} %reshape.1609), calls=%async_computation | async-start | bytes 98304 | tf_op jit(solution)/shard_map/all_to_all | solution.py:280
  181.0 7.5 %copy-start.4 = (f32[8,6,512]{2,0,1:T(8,128)S(1)}, f32[8,6,512]{2,0,1:T(8,128)}, u32[]{:S(2)}) copy-start(f32[8,6,512]{2,0,1:T(8,128)} %param.10) | copy-start | bytes 294916
  181.0 7.5 %copy-start.8 = (f32[384,512,1]{1,0,2:T(8,128)S(1)}, f32[384,512,1]{1,0,2:T(8,128)}, u32[]{:S(2)}) copy-start(f32[384,512,1]{1,0,2:T(8,128)} %constant.206) | copy-start | bytes 2359300
  181.0 7.5 %copy-start.11 = (f32[8,6,512]{2,0,1:T(8,128)S(1)}, f32[8,6,512]{2,0,1:T(8,128)}, u32[]{:S(2)}) copy-start(f32[8,6,512]{2,0,1:T(8,128)} %neg.17) | copy-start | bytes 294916
  181.0 7.5 %copy-start.51 = (f32[8]{0:T(128)S(1)}, f32[8]{0:T(128)}, u32[]{:S(2)}) copy-start(f32[8]{0:T(128)} %broadcast_multiply_fusion) | copy-start | bytes 100
  (29 other events, 59.5 us)
where the time goes:
time: 193 us; the launch traced here: 190 us
  local copies, waits for them, and re-layouts  72 us (37%)
  other arithmetic  51.2 us (27%)
  matrix products  45.3 us (23%)
  starting transfers between devices  20.5 us (11%)
    concatenate x20, local copies, waits for them, and re-layouts, state_parts(): jnp.concatenate([(density * speed_n)[:, None], momentum * speed_n[:, None...  33 us
    dot_general x1, matrix products, volume_term(): jnp.einsum('kc,evabc->evabk', deriv, fluxes[2], precision=highest)  22.2 us
    sub x4, other arithmetic, state_parts(): heat_ratio[:, None] - 1.0  14.2 us
    ppermute x4, starting transfers between devices, from_behind(): return lax.ppermute(block, axis, route)  13.3 us
    scatter-add x1, other arithmetic, section_update(): jax.ops.segment_sum(projected, mortar_info[0] * 6 + mortar_info[1], num_s...  7.32 us
    dot_general x1, matrix products, mortar_traces(): native = jnp.einsum('spq,svq->svp', operators, picked, precision=highest)  5.97 us
    neg x2, local copies, waits for them, and re-layouts, volume_term(): return -total.reshape(count_el, NV, VN)  5.9 us
    dot_general x1, matrix products, section_update(): jnp.einsum('spq,svp->svq', operators, correction, precision=highest)  4.5 us
  transfers between devices with their start and end apart: 6, of which 0 were waited for; matrix products, arithmetic and copies ran while one was open for 73% of the time, Pallas kernels for 0%

commit v1 on v0

v1 whole, which is shorter than its diff:
```python
import functools

import jax
import jax.numpy as jnp
import numpy as np
from jax import lax
from jax.experimental import pallas as pl
from jax.experimental.pallas import tpu as pltpu
from jax.sharding import PartitionSpec as P

NV = 6
FN = 64
CAPG = 8
CAPS = 32
TILE = 8
LANES = 128

step_size = 0.002
lift_weight = 49.0
MESH = pl.DeviceIdType.MESH
f32 = jnp.float32
bf16 = jnp.bfloat16


def cheb_matrix():
    points = -np.cos(np.pi * np.arange(8) / 7.0)
    factor = np.array([2.0, 1.0, 1.0, 1.0, 1.0, 1.0, 1.0, 2.0])
    alternating = np.where(np.arange(8) % 2 == 0, 1.0, -1.0)
    scaled = factor * alternating
    differ = points[:, None] - points[None, :] + np.eye(8)
    matrix = scaled[:, None] / scaled[None, :] / differ
    matrix = matrix * (1.0 - np.eye(8))
    return matrix - np.eye(8) * matrix.sum(axis=1)[:, None]


def plane_derivative():
    deriv_t = cheb_matrix().astype(np.float32).T
    both = np.concatenate(
        [np.kron(np.eye(16), deriv_t), np.kron(np.eye(2), np.kron(deriv_t, np.eye(8)))], axis=0
    ).astype(np.float32)
    high = both.astype(bf16)
    low = (both - high.astype(np.float32)).astype(bf16)
    return np.concatenate([high, low], axis=1)


def iota(shape, dim):
    return lax.broadcasted_iota(jnp.int32, shape, dim)


def split(x):
    high = x.astype(bf16).astype(f32)
    return high, x - high


def mm(a, b):
    return lax.dot_general(
        a.astype(bf16), b.astype(bf16), (((1,), (0,)), ((), ())), preferred_element_type=f32
    )


def mm_t(a, b):
    return lax.dot_general(
        a.astype(bf16), b.astype(bf16), (((1,), (1,)), ((), ())), preferred_element_type=f32
    )


def side(u, heat, normal):
    inverse = 1.0 / u[0]
    through = sum(n * m for n, m in zip(normal, u[1:4]) if n is not None)
    speed = through * inverse
    kinetic = 0.5 * (u[1] * u[1] + u[2] * u[2] + u[3] * u[3]) * inverse
    pressure = (heat - 1.0) * (u[4] - kinetic)
    return speed, pressure, jnp.sqrt(heat * pressure * inverse)


def flux_jump(own, other, own_heat, other_heat, normal):
    s_l, p_l, c_l = side(own, own_heat, normal)
    s_r, p_r, c_r = side(other, other_heat, normal)
    wave_l = jnp.minimum(s_l - c_l, s_r - c_r)
    wave_r = jnp.maximum(s_l + c_l, s_r + c_r)
    mass_l = own[0] * (wave_l - s_l)
    mass_r = other[0] * (wave_r - s_r)
    middle = (p_r - p_l + mass_l * s_l - mass_r * s_r) / (mass_l - mass_r)
    left = jnp.logical_or(wave_l >= 0.0, middle >= 0.0)
    u = [jnp.where(left, a, b) for a, b in zip(own, other)]
    s = jnp.where(left, s_l, s_r)
    p = jnp.where(left, p_l, p_r)
    wave = jnp.where(left, wave_l, wave_r)
    active = jnp.where(left, jnp.minimum(wave_l, 0.0), jnp.maximum(wave_r, 0.0))
    shifted = middle - s
    growth = shifted / (wave - middle)
    lifted = active * (growth + 1.0) * shifted
    scale = s + active * growth
    push = p_l - p - lifted * u[0]
    work = p_l * s_l - p * s - lifted * (u[0] * middle + p / (wave - s))
    jump = [s_l * a - scale * b for a, b in zip(own, u)]
    for d in range(3):
        if normal[d] is not None:
            jump[1 + d] = jump[1 + d] + normal[d] * push
    jump[4] = jump[4] + work
    return jump


def kernel(
    groups,
    ranks,
    material_ref,
    metric_ref,
    count_ref,
    state_ref,
    proj_ref,
    map_ref,
    nb_ref,
    deriv_ref,
    out_ref,
    send,
    recv,
    send_sem,
    recv_sem,
):
    elem = lax.axis_index("elem")
    grp = lax.axis_index("grp")
    has_up = elem + 1 < ranks
    has_down = elem > 0
    barrier = pltpu.get_barrier_semaphore()
    for off in range(1, groups):
        pl.semaphore_signal(
            barrier, inc=1, device_id=(elem, lax.rem(grp + off, groups)), device_id_type=MESH
        )

    @pl.when(has_up)
    def _():
        pl.semaphore_signal(barrier, inc=1, device_id=(elem + 1, grp), device_id_type=MESH)

    @pl.when(has_down)
    def _():
        pl.semaphore_signal(barrier, inc=1, device_id=(elem - 1, grp), device_id_type=MESH)

    slots = map_ref.shape[2]
    elems = state_ref.shape[0]
    nodes = state_ref.shape[2]
    blocks = slots // TILE
    chunks = nodes // LANES

    u = [state_ref[:, v, :] for v in range(NV)]
    heats = [1.4 + 0.27 * material_ref[j].astype(f32) for j in range(elems)]
    upper8 = iota((TILE, LANES), 1) >= FN
    col = iota((1, 256), 1)
    cell, far = col & 63, (col >> 6) & 1
    target = jnp.where(col < 128, 64 * (cell >> 3) + (cell & 7) + 56 * far, 8 * cell + 7 * far)
    pick_nodes = jnp.where(iota((nodes, 256), 0) == target, 1.0, 0.0).astype(bf16)
    high, low = split(jnp.concatenate(u, axis=0))
    both = mm(jnp.concatenate([high, low], axis=0), pick_nodes)
    flat = both[: NV * elems] + both[NV * elems :]
    trace = []
    for v in range(NV):
        rows = slice(v * elems, (v + 1) * elems)
        trace.append(
            [
                jnp.where(upper8, u[v][:, nodes - LANES :], u[v][:, :LANES]),
                flat[rows, :LANES],
                flat[rows, LANES:],
            ]
        )

    info = map_ref[0].astype(f32)
    same = iota((slots, slots), 0) == iota((slots, slots), 1)
    spread = mm(
        jnp.concatenate([jnp.where(same, info[i : i + 1], 0.0) for i in range(4)], axis=0),
        jnp.ones((slots, LANES), f32),
    ).astype(jnp.int32)
    owner, face, sub, orient = [spread[i * slots : (i + 1) * slots] for i in range(4)]
    half = jnp.where(iota((slots, LANES), 1) >= FN, 1, 0)
    upper = half == 1
    dim, end = face >> 1, face & 1

    cat = jnp.concatenate([t for ts in trace for t in ts], axis=1)
    high, low = split(cat)
    one_hot = jnp.where(owner[:, : 2 * elems] == (iota((slots, 2 * elems), 1) % elems), 1.0, 0.0)
    picked = mm(one_hot, jnp.concatenate([high, low], axis=0))
    at_end = end == half
    parts = []
    for v in range(NV):
        x, y, z = [
            picked[:, (3 * v + d) * LANES : (3 * v + d + 1) * LANES] for d in range(3)
        ]
        parts.append(jnp.where(at_end, jnp.where(dim == 0, x, jnp.where(dim == 1, y, z)), 0.0))

    col = iota((1, 512), 1)
    code, first, second = col >> 6, (col >> 3) & 7, col & 7
    swap = (code & 4) != 0
    first, second = jnp.where(swap, second, first), jnp.where(swap, first, second)
    first = jnp.where((code & 1) != 0, 7 - first, first)
    second = jnp.where((code & 2) != 0, 7 - second, second)
    turn = jnp.where((iota((LANES, 512), 0) & 63) == 8 * first + second, 1.0, 0.0).astype(bf16)
    high, low = split(jnp.concatenate(parts, axis=0))
    turned = mm(
        jnp.concatenate([high, low], axis=1), jnp.concatenate([turn, turn], axis=0)
    )
    pair = orient >> 1
    in_place = (orient & 1) == half
    parts = []
    for v in range(NV):
        a, b, c, d = [
            turned[v * slots : (v + 1) * slots, i * LANES : (i + 1) * LANES] for i in range(4)
        ]
        x = jnp.where(pair == 0, a, jnp.where(pair == 1, b, jnp.where(pair == 2, c, d)))
        parts.append(jnp.where(in_place, x, pltpu.roll(x, FN, 1)))

    quads = proj_ref[...].reshape(4 * FN, FN)
    quad_high, quad_low = split(quads)
    lhs_a, lhs_b = [], []
    for v in range(NV):
        high, low = split(parts[v])
        lhs_a.append(jnp.where(upper, low, high))
        lhs_b.append(jnp.where(upper, 0.0, high))
    projected = mm_t(
        jnp.concatenate([jnp.concatenate(lhs_a, axis=0), jnp.concatenate(lhs_b, axis=0)], axis=1),
        jnp.concatenate([quad_high, quad_high, quad_low, jnp.zeros_like(quad_low)], axis=1),
    )
    in_place = (sub & 1) != half
    native = []
    for v in range(NV):
        rows = slice(v * slots, (v + 1) * slots)
        x = jnp.where(sub >= 3, projected[rows, LANES:], projected[rows, :LANES])
        x = jnp.where(in_place, x, pltpu.roll(x, FN, 1))
        native.append(jnp.where(sub == 0, parts[v], x))
    native_heat = jnp.full((slots, LANES), heats[0], f32)
    for j in range(1, elems):
        native_heat = jnp.where(owner == j, heats[j], native_heat)

    for i in range(3):
        plane = jnp.where(upper, native[2 * i + 1], native[2 * i])
        send[:, i] = plane.reshape(blocks, TILE, LANES)
    send[:, 3] = native_heat.reshape(blocks, TILE, LANES)
    many = CAPS // TILE
    up_at, down_at = pl.ds(groups, many), pl.ds(groups + many, many)

    def to_peer(off):
        peer = lax.rem(grp + off, groups)
        return pltpu.make_async_remote_copy(
            src_ref=send.at[peer],
            dst_ref=recv.at[grp],
            send_sem=send_sem.at[off],
            recv_sem=recv_sem.at[off],
            device_id=(elem, peer),
            device_id_type=MESH,
        )

    def from_peer(off):
        peer = lax.rem(grp + groups - off, groups)
        return pltpu.make_async_remote_copy(
            src_ref=send.at[peer],
            dst_ref=recv.at[peer],
            send_sem=send_sem.at[off],
            recv_sem=recv_sem.at[off],
            device_id=(elem, peer),
            device_id_type=MESH,
        )

    def along(src, dst, sem, step):
        return pltpu.make_async_remote_copy(
            src_ref=send.at[src],
            dst_ref=recv.at[dst],
            send_sem=send_sem.at[sem],
            recv_sem=recv_sem.at[sem],
            device_id=(elem + step, grp),
            device_id_type=MESH,
        )

    up_sem, down_sem = groups, groups + 1
    pl.semaphore_wait(
        barrier, groups - 1 + has_up.astype(jnp.int32) + has_down.astype(jnp.int32)
    )

    @pl.when(has_up)
    def _():
        along(up_at, down_at, up_sem, 1).start()

    @pl.when(has_down)
    def _():
        along(down_at, up_at, down_sem, -1).start()

    for off in range(1, groups):
        to_peer(off).start()

    row8 = iota((TILE, LANES), 0)
    heat = jnp.full((TILE, LANES), heats[0], f32)
    for j in range(1, elems):
        heat = jnp.where(row8 == j, heats[j], heat)
    sign = jnp.where(upper8, 1.0, -1.0)
    across_all = nb_ref[...]
    local = []
    for d in range(3):
        across = jnp.where(
            upper8, across_all[:, 2 * d + 1 : 2 * d + 2], across_all[:, 2 * d : 2 * d + 1]
        )
        own = [trace[v][d] for v in range(NV)]
        opposite = [pltpu.roll(x, FN, 1) for x in own]
        other, other_heat = own, heat
        for j in range(elems):
            here = across == j
            other = [jnp.where(here, o[j : j + 1], x) for o, x in zip(opposite, other)]
            other_heat = jnp.where(here, heats[j], other_heat)
        normal = [None, None, None]
        normal[d] = sign
        jump = flux_jump(own, other, heat, other_heat, normal)
        local.append([jnp.where(across >= 0, x, 0.0) for x in jump])

    heat_all = jnp.concatenate([heat] * chunks, axis=1)
    inverse = 1.0 / u[0]
    velocity = [u[1 + d] * inverse for d in range(3)]
    kinetic = 0.5 * (u[1] * velocity[0] + u[2] * velocity[1] + u[3] * velocity[2])
    pressure = (heat_all - 1.0) * (u[4] - kinetic)

    def flux(d):
        s = velocity[d]
        f = [u[1 + d]] + [m * s for m in u[1:4]] + [(u[4] + pressure) * s, u[5] * s]
        f[1 + d] = f[1 + d] + pressure
        return f

    def cut(x):
        return [x[:, i * LANES : (i + 1) * LANES] for i in range(chunks)]

    deriv = cheb_matrix()
    flux_x, flux_y, flux_z = [[cut(f) for f in flux(d)] for d in range(3)]
    stacked = jnp.concatenate(
        [
            jnp.concatenate([flux_z[v][i], flux_y[v][i]], axis=1)
            for v in range(NV)
            for i in range(chunks)
        ],
        axis=0,
    )
    high, low = split(stacked)
    rows = NV * chunks * TILE
    both = mm(jnp.concatenate([high, low], axis=0), deriv_ref[...])
    plane_sum = both[:rows, :LANES] + both[:rows, LANES:] + both[rows:, :LANES]
    rolled_x = [[pltpu.roll(x, FN, 1) for x in flux_x[v]] for v in range(NV)]
    volume = [[None] * chunks for _ in range(NV)]
    for j in range(chunks):
        weights = []
        for i in range(chunks):
            straight = jnp.where(
                upper8, float(deriv[2 * j + 1, 2 * i + 1]), float(deriv[2 * j, 2 * i])
            )
            crossed = jnp.where(
                upper8, float(deriv[2 * j + 1, 2 * i]), float(deriv[2 * j, 2 * i + 1])
            )
            weights.append((straight, crossed))
        for v in range(NV):
            at = (v * chunks + j) * TILE
            total = plane_sum[at : at + TILE]
            for i in range(chunks):
                total = total + weights[i][0] * flux_x[v][i] + weights[i][1] * rolled_x[v][i]
            volume[v][j] = -total

    row = iota((TILE, LANES), 0)
    live = [row < count_ref[0, g] for g in range(groups)]
    for side_at in (groups, groups + 1):
        live += [row + TILE * i < count_ref[0, side_at] for i in range(many)]
    live = jnp.concatenate([jnp.where(x, 1.0, 0.0) for x in live], axis=0) > 0.0
    sign = jnp.where(end == 1, 1.0, -1.0)
    normal = [jnp.where(dim == d, sign, 0.0) for d in range(3)]
    back_weight = jnp.where(sub == 0, 1.0, 0.25)

    for off in range(1, groups):
        from_peer(off).wait_recv()

    @pl.when(has_up)
    def _():
        along(down_at, up_at, down_sem, 1).wait_recv()

    @pl.when(has_down)
    def _():
        along(up_at, down_at, up_sem, -1).wait_recv()

    partner = []
    for i in range(3):
        plane = recv[:, i].reshape(slots, LANES)
        moved = pltpu.roll(plane, FN, 1)
        partner += [jnp.where(upper, moved, plane), jnp.where(upper, plane, moved)]
    partner = [jnp.where(live, a, b) for a, b in zip(partner, native)]
    partner_heat = jnp.where(live, recv[:, 3].reshape(slots, LANES), native_heat)
    jump = flux_jump(native, partner, native_heat, partner_heat, normal)
    corr = [jnp.where(live, back_weight * x, 0.0) for x in jump]

    in_a, in_b = sub == 1 + half, sub == 3 + half
    highs, lows = [], []
    for v in range(NV):
        high, low = split(corr[v])
        for kept, x in ((highs, high), (lows, low)):
            kept.append(
                jnp.concatenate([jnp.where(in_a, x, 0.0), jnp.where(in_b, x, 0.0)], axis=1)
            )
    both = mm(
        jnp.concatenate(highs + lows, axis=0),
        jnp.concatenate([quad_high, quad_high, quad_low, quad_low], axis=1),
    )
    lhs_high, lhs_low = [], []
    for v in range(NV):
        h = both[v * slots : (v + 1) * slots]
        l = both[(NV + v) * slots : (NV + v + 1) * slots]
        x = jnp.where(sub == 0, corr[v], h[:, :LANES] + h[:, LANES:] + l[:, :LANES])
        high, low = split(x)
        for kept, y in ((lhs_high, high), (lhs_low, low)):
            kept.append(
                jnp.concatenate(
                    [jnp.where(orient == 2 * i + half, y, 0.0) for i in range(4)], axis=1
                )
            )
    both = mm_t(jnp.concatenate(lhs_high + lhs_low, axis=0), turn)
    placed = []
    for v in range(NV):
        x = both[v * slots : (v + 1) * slots] + both[(NV + v) * slots : (NV + v + 1) * slots]
        x = jnp.where(at_end, x, 0.0)
        placed += [jnp.where(dim == d, x, 0.0) for d in range(3)]
    high, low = split(jnp.concatenate(placed, axis=1))
    gather = jnp.where(iota((elems, slots), 0) == map_ref[0, 0:1, :], 1.0, 0.0)
    face_sum = mm(gather, high) + mm(gather, low)

    lines = []
    for v in range(NV):
        at = 3 * v * LANES
        lines.append([face_sum[:, at + d * LANES : at + (d + 1) * LANES] + local[d][v] for d in range(3)])
    wide = jnp.concatenate([jnp.concatenate(x[1:], axis=1) for x in lines], axis=0)
    high, low = split(wide)
    both = mm_t(jnp.concatenate([high, low], axis=0), pick_nodes)
    surface = both[: NV * elems] + both[NV * elems :]
    scale = jnp.full((TILE, LANES), metric_ref[0], f32)
    for j in range(1, elems):
        scale = jnp.where(row8 == j, metric_ref[j], scale)
    scale = step_size * scale
    for v in range(NV):
        for j in range(chunks):
            s = surface[v * elems : (v + 1) * elems, j * LANES : (j + 1) * LANES]
            if j == 0:
                s = s + jnp.where(upper8, 0.0, lines[v][0])
            if j == chunks - 1:
                s = s + jnp.where(upper8, lines[v][0], 0.0)
            at = slice(j * LANES, (j + 1) * LANES)
            out_ref[:, v, at] = u[v][:, at] + scale * (volume[v][j] + lift_weight * s)

    for off in range(1, groups):
        to_peer(off).wait_send()

    @pl.when(has_up)
    def _():
        along(up_at, down_at, up_sem, 1).wait_send()

    @pl.when(has_down)
    def _():
        along(down_at, up_at, down_sem, -1).wait_send()


def shards(state, material, metric, mortar_proj, mortar_map, mortar_count, neighbours):
    groups, ranks = lax.axis_size("grp"), lax.axis_size("elem")
    blocks = mortar_map.shape[2] // TILE
    vmem = pl.BlockSpec(memory_space=pltpu.VMEM)
    smem = pl.BlockSpec(memory_space=pltpu.SMEM)
    return pl.pallas_call(
        functools.partial(kernel, groups, ranks),
        out_shape=jax.ShapeDtypeStruct(state.shape, state.dtype),
        in_specs=[smem] * 3 + [vmem] * 5,
        out_specs=vmem,
        scratch_shapes=[
            pltpu.VMEM((blocks, 4, TILE, LANES), f32),
            pltpu.VMEM((blocks, 4, TILE, LANES), f32),
            pltpu.SemaphoreType.DMA((groups + 2,)),
            pltpu.SemaphoreType.DMA((groups + 2,)),
        ],
        compiler_params=pltpu.CompilerParams(
            collective_id=0, has_side_effects=True, vmem_limit_bytes=40 * 2**20
        ),
    )(
        material,
        metric,
        mortar_count,
        state,
        mortar_proj,
        mortar_map,
        neighbours,
        jnp.asarray(plane_derivative()),
    )


def solution(mesh):
    return jax.shard_map(
        shards,
        mesh=mesh,
        in_specs=(
            P(("elem", "grp"), None, None),
            P(("elem", "grp")),
            P(("elem", "grp")),
            P(),
            P(("elem", "grp"), None, None),
            P(("elem", "grp"), None),
            P(("elem", "grp"), None),
        ),
        out_specs=P(("elem", "grp"), None, None),
        check_vma=False,
    )
```

time: 193 us -> 12.3 us (0.06); the launches traced: 190 us -> 12.1 us
  local copies, waits for them, and re-layouts: 72 us -> 2.65 us
  other arithmetic: 51.2 us -> 0 us
  matrix products: 45.3 us -> 0 us
  starting transfers between devices: 20.5 us -> 0 us
  Pallas kernels: 0 us -> 9.33 us
    dot_general x8 -> x0, matrix products: 45.3 us -> none  [the longest x1 22.2 us: volume_term(): jnp.einsum('kc,evabc->evabk', deriv, fluxes[2], precision=highest)]
    concatenate x21 -> x0, local copies, waits for them, and re-layouts: 33.1 us -> none  [the longest x20 33 us: state_parts(): jnp.concatenate([(density * speed_n)[:, None], momentum * speed_n[:, None...]
    sub x4 -> x0, other arithmetic: 14.2 us -> none  [state_parts(): heat_ratio[:, None] - 1.0]
    ppermute x4 -> x0, starting transfers between devices: 13.3 us -> none  [from_behind(): return lax.ppermute(block, axis, route)]
    reshape x12 -> x0, local copies, waits for them, and re-layouts: 10.5 us -> none  [the longest x2 1.75 us: shards(): arrived = arrived.reshape(grp_slots, NV, FN)]
    pallas_call x0 -> x1, Pallas kernels: none -> 9.33 us  [shards(): pl.pallas_call(functools.partial(kernel, groups, ranks), out_shape=jax.Sh...]
    select_n x13 -> x0, other arithmetic: 8.92 us -> none  [the longest x1 1.43 us: mortar_traces(): picked = face_rows[mortar_info[0] * 6 + mortar_info[1]]]
    scatter-add x1 -> x0, other arithmetic: 7.32 us -> none  [section_update(): jax.ops.segment_sum(projected, mortar_info[0] * 6 + mortar_info[1], num_s...]
  transfers between devices with their start and end apart: 6 -> 0, of which waited for: 0 -> 0; matrix products, arithmetic and copies ran while one was open for 73% -> 0% of each run, Pallas kernels for 0% -> 0%
where the time goes in v1:
time: 12.3 us; the launch traced here: 12.1 us
  Pallas kernels  9.33 us (76%)
  local copies, waits for them, and re-layouts  2.65 us (22%)
    pallas_call x1, Pallas kernels, shards(): pl.pallas_call(functools.partial(kernel, groups, ranks), out_shape=jax.Sh...  9.33 us
    unnamed x15, local copies, waits for them, and re-layouts  1.95 us
    pallas_call x1, local copies, waits for them, and re-layouts, shards(): pl.pallas_call(functools.partial(kernel, groups, ranks), out_shape=jax.Sh...  0.7 us

profile of v1, /device:TPU:0, one launch (start us, length us, event | category | flops | bytes accessed | tf_op | source)
XLA Modules:
  0.0 12.1 jit_solution(250695686813462767)
XLA Ops:
  0.0 0.0 copy-start.2
  0.0 0.0 copy-start.6
  0.0 0.0 copy-start.3
  0.0 0.0 copy-start
  0.0 0.0 copy-start.5
  0.0 0.0 copy-start.4
  0.0 1.0 %copy.9.state_ref = f32[8,6,512]{2,1,0:T(8,128)S(1)} copy(f32[8,6,512]{2,0,1:T(8,128)} %param.8) | data formatting | bytes 196608 | tf_op args[0]
  1.0 0.0 copy-done.2
  1.1 0.0 copy-done.6
  1.1 0.0 copy-done.3
  1.1 0.0 copy-done
  1.1 0.0 copy-done.5
  1.1 0.0 copy-done.4
  1.1 0.0 copy-start.1
  1.1 0.9 %copy-done.1 = bf16[256,256]{1,0:T(8,128)(2,1)S(1)} copy-done((bf16[256,256]{1,0:T(8,128)(2,1)S(1)}, bf16[256,256]{1,0:T(8,128)(2,1)}, u32[]{:S(2)}) %copy-start.1) | copy-done | bytes 131096
  2.0 9.3 %shard_map.82 = f32[8,6,512]{2,1,0:T(8,128)S(1)} custom-call(s32[8]{0:T(128)S(1)} %copy-done.4, f32[8]{0:T(128)S(1)} %copy-done.5, s32[1,6]{1,0:T(1,128)S(1)} %copy-done.6, f32[8,6,512]{2,1,0:T(8,128)S(1)} %copy.9.state_ref, f32[4,64,64]{2,1,0:T(8,128)S(1)} %copy-done, s32[1,4,96]{2,1,0:T(4,128)S(1)} %copy-done.3, s32[8,6]{1,0:T(8,128)S(1)} %copy-done.2, ...), custom_call_target="tpu_custom_call" | custom-call | tf_op jit(solution)/shard_map/pallas_call | solution.py:461
  11.4 0.7 %copy.10 = f32[8,6,512]{2,0,1:T(8,128)} copy(f32[8,6,512]{2,1,0:T(8,128)S(1)} %shard_map.82) | data formatting | bytes 196608 | tf_op jit(solution)/shard_map/pallas_call | solution.py:461
Async XLA Ops:
  0.0 1.1 %copy-start.2 = (s32[8,6]{1,0:T(8,128)S(1)}, s32[8,6]{1,0:T(8,128)}, u32[]{:S(2)}) copy-start(s32[8,6]{1,0:T(8,128)} %nb_ref.1) | copy-start | bytes 580
  0.0 1.1 %copy-start.6 = (s32[1,6]{1,0:T(1,128)S(1)}, s32[1,6]{1,0:T(1,128)}, u32[]{:S(2)}) copy-start(s32[1,6]{1,0:T(1,128)} %count_ref.1) | copy-start | bytes 76
  0.0 1.1 %copy-start.3 = (s32[1,4,96]{2,1,0:T(4,128)S(1)}, s32[1,4,96]{2,1,0:T(4,128)}, u32[]{:S(2)}) copy-start(s32[1,4,96]{2,1,0:T(4,128)} %map_ref.1) | copy-start | bytes 4612
  0.0 1.1 %copy-start = (f32[4,64,64]{2,1,0:T(8,128)S(1)}, f32[4,64,64]{2,1,0:T(8,128)}, u32[]{:S(2)}) copy-start(f32[4,64,64]{2,1,0:T(8,128)} %proj_ref.1) | copy-start | bytes 196612
  0.0 1.1 %copy-start.5 = (f32[8]{0:T(128)S(1)}, f32[8]{0:T(128)}, u32[]{:S(2)}) copy-start(f32[8]{0:T(128)} %metric_ref.1) | copy-start | bytes 100
  0.0 1.1 %copy-start.4 = (s32[8]{0:T(128)S(1)}, s32[8]{0:T(128)}, u32[]{:S(2)}) copy-start(s32[8]{0:T(128)} %material_ref.1) | copy-start | bytes 100
  1.1 0.9 %copy-start.1 = (bf16[256,256]{1,0:T(8,128)(2,1)S(1)}, bf16[256,256]{1,0:T(8,128)(2,1)}, u32[]{:S(2)}) copy-start(bf16[256,256]{1,0:T(8,128)(2,1)} %constant.2.clone.deriv_ref) | copy-start | bytes 393220

commit v2 on v1

--- a/solution.py
+++ b/solution.py
@@ -101,23 +101,86 @@
     return jump
 
 
+def chosen_turn(turned, orient, half):
+    slots = orient.shape[0]
+    pair = orient >> 1
+    in_place = (orient & 1) == half
+    result = []
+    for v in range(NV):
+        a, b, c, d = [
+            turned[v * slots : (v + 1) * slots, i * LANES : (i + 1) * LANES] for i in range(4)
+        ]
+        x = jnp.where(pair == 0, a, jnp.where(pair == 1, b, jnp.where(pair == 2, c, d)))
+        result.append(jnp.where(in_place, x, pltpu.roll(x, FN, 1)))
+    return result
+
+
+def split_columns(parts, upper):
+    first, second = [], []
+    for x in parts:
+        high, low = split(x)
+        first.append(jnp.where(upper, low, high))
+        second.append(jnp.where(upper, 0.0, high))
+    return jnp.concatenate(
+        [jnp.concatenate(first, axis=0), jnp.concatenate(second, axis=0)], axis=1
+    )
+
+
+def chosen_quad(projected, parts, sub, half):
+    slots = sub.shape[0]
+    in_place = (sub & 1) != half
+    result = []
+    for v in range(NV):
+        rows = slice(v * slots, (v + 1) * slots)
+        x = jnp.where(sub >= 3, projected[rows, LANES:], projected[rows, :LANES])
+        x = jnp.where(in_place, x, pltpu.roll(x, FN, 1))
+        result.append(jnp.where(sub == 0, parts[v], x))
+    return result
+
+
 def kernel(
     groups,
     ranks,
+    state_hbm,
+    map_hbm,
+    material_hbm,
+    proj_hbm,
+    nb_hbm,
+    count_hbm,
+    metric_hbm,
+    deriv_hbm,
+    out_ref,
+    state_ref,
+    map_ref,
     material_ref,
+    proj_ref,
+    nb_ref,
+    count_ref,
     metric_ref,
-    count_ref,
-    state_ref,
-    proj_ref,
-    map_ref,
-    nb_ref,
     deriv_ref,
-    out_ref,
     send,
     recv,
     send_sem,
     recv_sem,
+    fetch_sem,
 ):
+    fetches = [
+        pltpu.make_async_copy(src, dst, fetch_sem.at[i])
+        for i, (src, dst) in enumerate(
+            (
+                (state_hbm, state_ref),
+                (map_hbm, map_ref),
+                (material_hbm, material_ref),
+                (proj_hbm, proj_ref),
+                (nb_hbm, nb_ref),
+                (count_hbm, count_ref),
+                (metric_hbm, metric_ref),
+                (deriv_hbm, deriv_ref),
+            )
+        )
+    ]
+    for fetch in fetches:
+        fetch.start()
     elem = lax.axis_index("elem")
     grp = lax.axis_index("grp")
     has_up = elem + 1 < ranks
@@ -137,18 +200,28 @@
         pl.semaphore_signal(barrier, inc=1, device_id=(elem - 1, grp), device_id_type=MESH)
 
     slots = map_ref.shape[2]
-    elems = state_ref.shape[0]
+    elems = state_ref.shape[1]
     nodes = state_ref.shape[2]
     blocks = slots // TILE
     chunks = nodes // LANES
 
-    u = [state_ref[:, v, :] for v in range(NV)]
-    heats = [1.4 + 0.27 * material_ref[j].astype(f32) for j in range(elems)]
     upper8 = iota((TILE, LANES), 1) >= FN
     col = iota((1, 256), 1)
     cell, far = col & 63, (col >> 6) & 1
     target = jnp.where(col < 128, 64 * (cell >> 3) + (cell & 7) + 56 * far, 8 * cell + 7 * far)
     pick_nodes = jnp.where(iota((nodes, 256), 0) == target, 1.0, 0.0).astype(bf16)
+    col = iota((1, 512), 1)
+    code, first, second = col >> 6, (col >> 3) & 7, col & 7
+    swap = (code & 4) != 0
+    first, second = jnp.where(swap, second, first), jnp.where(swap, first, second)
+    first = jnp.where((code & 1) != 0, 7 - first, first)
+    second = jnp.where((code & 2) != 0, 7 - second, second)
+    turn = jnp.where((iota((LANES, 512), 0) & 63) == 8 * first + second, 1.0, 0.0).astype(bf16)
+    same = iota((slots, slots), 0) == iota((slots, slots), 1)
+    for fetch in fetches[:3]:
+        fetch.wait()
+    u = [state_ref[v] for v in range(NV)]
+    heats = [1.4 + 0.27 * material_ref[j].astype(f32) for j in range(elems)]
     high, low = split(jnp.concatenate(u, axis=0))
     both = mm(jnp.concatenate([high, low], axis=0), pick_nodes)
     flat = both[: NV * elems] + both[NV * elems :]
@@ -164,7 +237,6 @@
         )
 
     info = map_ref[0].astype(f32)
-    same = iota((slots, slots), 0) == iota((slots, slots), 1)
     spread = mm(
         jnp.concatenate([jnp.where(same, info[i : i + 1], 0.0) for i in range(4)], axis=0),
         jnp.ones((slots, LANES), f32),
@@ -174,57 +246,34 @@
     upper = half == 1
     dim, end = face >> 1, face & 1
 
-    cat = jnp.concatenate([t for ts in trace for t in ts], axis=1)
-    high, low = split(cat)
-    one_hot = jnp.where(owner[:, : 2 * elems] == (iota((slots, 2 * elems), 1) % elems), 1.0, 0.0)
+    high, low = split(
+        jnp.concatenate(
+            [jnp.concatenate([trace[v][d] for v in range(NV)], axis=1) for d in range(3)], axis=0
+        )
+    )
+    rows = 3 * elems
+    place = dim * elems + owner
+    one_hot = jnp.where(place[:, : 2 * rows] == (iota((slots, 2 * rows), 1) % rows), 1.0, 0.0)
     picked = mm(one_hot, jnp.concatenate([high, low], axis=0))
     at_end = end == half
-    parts = []
-    for v in range(NV):
-        x, y, z = [
-            picked[:, (3 * v + d) * LANES : (3 * v + d + 1) * LANES] for d in range(3)
-        ]
-        parts.append(jnp.where(at_end, jnp.where(dim == 0, x, jnp.where(dim == 1, y, z)), 0.0))
-
-    col = iota((1, 512), 1)
-    code, first, second = col >> 6, (col >> 3) & 7, col & 7
-    swap = (code & 4) != 0
-    first, second = jnp.where(swap, second, first), jnp.where(swap, first, second)
-    first = jnp.where((code & 1) != 0, 7 - first, first)
-    second = jnp.where((code & 2) != 0, 7 - second, second)
-    turn = jnp.where((iota((LANES, 512), 0) & 63) == 8 * first + second, 1.0, 0.0).astype(bf16)
+    parts = [
+        jnp.where(at_end, picked[:, v * LANES : (v + 1) * LANES], 0.0) for v in range(NV)
+    ]
+
     high, low = split(jnp.concatenate(parts, axis=0))
     turned = mm(
         jnp.concatenate([high, low], axis=1), jnp.concatenate([turn, turn], axis=0)
     )
-    pair = orient >> 1
-    in_place = (orient & 1) == half
-    parts = []
-    for v in range(NV):
-        a, b, c, d = [
-            turned[v * slots : (v + 1) * slots, i * LANES : (i + 1) * LANES] for i in range(4)
-        ]
-        x = jnp.where(pair == 0, a, jnp.where(pair == 1, b, jnp.where(pair == 2, c, d)))
-        parts.append(jnp.where(in_place, x, pltpu.roll(x, FN, 1)))
-
+    parts = chosen_turn(turned, orient, half)
+
+    fetches[3].wait()
     quads = proj_ref[...].reshape(4 * FN, FN)
     quad_high, quad_low = split(quads)
-    lhs_a, lhs_b = [], []
-    for v in range(NV):
-        high, low = split(parts[v])
-        lhs_a.append(jnp.where(upper, low, high))
-        lhs_b.append(jnp.where(upper, 0.0, high))
     projected = mm_t(
-        jnp.concatenate([jnp.concatenate(lhs_a, axis=0), jnp.concatenate(lhs_b, axis=0)], axis=1),
+        split_columns(parts, upper),
         jnp.concatenate([quad_high, quad_high, quad_low, jnp.zeros_like(quad_low)], axis=1),
     )
-    in_place = (sub & 1) != half
-    native = []
-    for v in range(NV):
-        rows = slice(v * slots, (v + 1) * slots)
-        x = jnp.where(sub >= 3, projected[rows, LANES:], projected[rows, :LANES])
-        x = jnp.where(in_place, x, pltpu.roll(x, FN, 1))
-        native.append(jnp.where(sub == 0, parts[v], x))
+    native = chosen_quad(projected, parts, sub, half)
     native_heat = jnp.full((slots, LANES), heats[0], f32)
     for j in range(1, elems):
         native_heat = jnp.where(owner == j, heats[j], native_heat)
@@ -284,6 +333,8 @@
     for off in range(1, groups):
         to_peer(off).start()
 
+    for fetch in fetches[4:]:
+        fetch.wait()
     row8 = iota((TILE, LANES), 0)
     heat = jnp.full((TILE, LANES), heats[0], f32)
     for j in range(1, elems):
@@ -363,6 +414,14 @@
     sign = jnp.where(end == 1, 1.0, -1.0)
     normal = [jnp.where(dim == d, sign, 0.0) for d in range(3)]
     back_weight = jnp.where(sub == 0, 1.0, 0.25)
+    across_quads = jnp.concatenate([proj_ref[i] for i in range(4)], axis=1)
+    quad_high, quad_low = split(across_quads)
+    quads_back = jnp.concatenate(
+        [quad_high, quad_high, quad_low, jnp.zeros_like(quad_low)], axis=0
+    ).astype(bf16)
+    back_orient = jnp.where(orient >= 5, jnp.where(orient == 7, 7, 11 - orient), orient)
+    gather_at = (map_ref[0, 1:2, :] >> 1) * elems + map_ref[0, 0:1, :]
+    gather = jnp.where(iota((3 * elems, slots), 0) == gather_at, 1.0, 0.0).astype(bf16)
 
     for off in range(1, groups):
         from_peer(off).wait_recv()
@@ -385,44 +444,23 @@
     jump = flux_jump(native, partner, native_heat, partner_heat, normal)
     corr = [jnp.where(live, back_weight * x, 0.0) for x in jump]
 
-    in_a, in_b = sub == 1 + half, sub == 3 + half
-    highs, lows = [], []
-    for v in range(NV):
-        high, low = split(corr[v])
-        for kept, x in ((highs, high), (lows, low)):
-            kept.append(
-                jnp.concatenate([jnp.where(in_a, x, 0.0), jnp.where(in_b, x, 0.0)], axis=1)
-            )
-    both = mm(
-        jnp.concatenate(highs + lows, axis=0),
-        jnp.concatenate([quad_high, quad_high, quad_low, quad_low], axis=1),
-    )
-    lhs_high, lhs_low = [], []
-    for v in range(NV):
-        h = both[v * slots : (v + 1) * slots]
-        l = both[(NV + v) * slots : (NV + v + 1) * slots]
-        x = jnp.where(sub == 0, corr[v], h[:, :LANES] + h[:, LANES:] + l[:, :LANES])
+    parts = chosen_quad(mm(split_columns(corr, upper), quads_back), corr, sub, half)
+    lhs = []
+    for x in parts:
         high, low = split(x)
-        for kept, y in ((lhs_high, high), (lhs_low, low)):
-            kept.append(
-                jnp.concatenate(
-                    [jnp.where(orient == 2 * i + half, y, 0.0) for i in range(4)], axis=1
-                )
-            )
-    both = mm_t(jnp.concatenate(lhs_high + lhs_low, axis=0), turn)
-    placed = []
-    for v in range(NV):
-        x = both[v * slots : (v + 1) * slots] + both[(NV + v) * slots : (NV + v + 1) * slots]
-        x = jnp.where(at_end, x, 0.0)
-        placed += [jnp.where(dim == d, x, 0.0) for d in range(3)]
-    high, low = split(jnp.concatenate(placed, axis=1))
-    gather = jnp.where(iota((elems, slots), 0) == map_ref[0, 0:1, :], 1.0, 0.0)
+        lhs.append(jnp.where(upper, low, high))
+    parts = chosen_turn(mm(jnp.concatenate(lhs, axis=0), turn), back_orient, half)
+    high, low = split(
+        jnp.concatenate([jnp.where(at_end, x, 0.0) for x in parts], axis=1)
+    )
     face_sum = mm(gather, high) + mm(gather, low)
 
     lines = []
     for v in range(NV):
-        at = 3 * v * LANES
-        lines.append([face_sum[:, at + d * LANES : at + (d + 1) * LANES] + local[d][v] for d in range(3)])
+        at = slice(v * LANES, (v + 1) * LANES)
+        lines.append(
+            [face_sum[d * elems : (d + 1) * elems, at] + local[d][v] for d in range(3)]
+        )
     wide = jnp.concatenate([jnp.concatenate(x[1:], axis=1) for x in lines], axis=0)
     high, low = split(wide)
     both = mm_t(jnp.concatenate([high, low], axis=0), pick_nodes)
@@ -439,7 +477,7 @@
             if j == chunks - 1:
                 s = s + jnp.where(upper8, lines[v][0], 0.0)
             at = slice(j * LANES, (j + 1) * LANES)
-            out_ref[:, v, at] = u[v][:, at] + scale * (volume[v][j] + lift_weight * s)
+            out_ref[v, :, at] = u[v][:, at] + scale * (volume[v][j] + lift_weight * s)
 
     for off in range(1, groups):
         to_peer(off).wait_send()
@@ -456,32 +494,39 @@
 def shards(state, material, metric, mortar_proj, mortar_map, mortar_count, neighbours):
     groups, ranks = lax.axis_size("grp"), lax.axis_size("elem")
     blocks = mortar_map.shape[2] // TILE
-    vmem = pl.BlockSpec(memory_space=pltpu.VMEM)
-    smem = pl.BlockSpec(memory_space=pltpu.SMEM)
-    return pl.pallas_call(
+    by_variable = jnp.transpose(state, (1, 0, 2))
+    operands = (
+        by_variable,
+        mortar_map,
+        material,
+        mortar_proj,
+        neighbours,
+        mortar_count,
+        metric,
+        jnp.asarray(plane_derivative()),
+    )
+    in_smem = (2, 5, 6)
+    result = pl.pallas_call(
         functools.partial(kernel, groups, ranks),
-        out_shape=jax.ShapeDtypeStruct(state.shape, state.dtype),
-        in_specs=[smem] * 3 + [vmem] * 5,
-        out_specs=vmem,
+        out_shape=jax.ShapeDtypeStruct(by_variable.shape, state.dtype),
+        in_specs=[pl.BlockSpec(memory_space=pltpu.HBM)] * len(operands),
+        out_specs=pl.BlockSpec(memory_space=pltpu.VMEM),
         scratch_shapes=[
+            (pltpu.SMEM if i in in_smem else pltpu.VMEM)(x.shape, x.dtype)
+            for i, x in enumerate(operands)
+        ]
+        + [
             pltpu.VMEM((blocks, 4, TILE, LANES), f32),
             pltpu.VMEM((blocks, 4, TILE, LANES), f32),
             pltpu.SemaphoreType.DMA((groups + 2,)),
             pltpu.SemaphoreType.DMA((groups + 2,)),
+            pltpu.SemaphoreType.DMA((len(operands),)),
         ],
         compiler_params=pltpu.CompilerParams(
-            collective_id=0, has_side_effects=True, vmem_limit_bytes=40 * 2**20
+            collective_id=0, has_side_effects=True, vmem_limit_bytes=56 * 2**20
         ),
-    )(
-        material,
-        metric,
-        mortar_count,
-        state,
-        mortar_proj,
-        mortar_map,
-        neighbours,
-        jnp.asarray(plane_derivative()),
-    )
+    )(*operands)
+    return jnp.transpose(result, (1, 0, 2))
 
 
 def solution(mesh):

time: 12.3 us -> 10.9 us (0.89)
  local copies, waits for them, and re-layouts: 2.65 us -> 1.54 us
  Pallas kernels: 9.33 us -> 9.2 us
    pallas_call x1 -> x0, local copies, waits for them, and re-layouts: 0.7 us -> none  [shards(): pl.pallas_call(functools.partial(kernel, groups, ranks), out_shape=jax.Sh...]
    unnamed x15 -> x1, local copies, waits for them, and re-layouts: 1.95 us -> 1.54 us
    pallas_call x1, Pallas kernels: 9.33 us -> 9.2 us  [shards(): pl.pallas_call(functools.partial(kernel, groups, ranks), out_shape=jax.Sh...]
where the time goes in v2:
time: 10.9 us; the launch traced here: 10.7 us
  Pallas kernels  9.2 us (84%)
  local copies, waits for them, and re-layouts  1.54 us (14%)
    pallas_call x1, Pallas kernels, shards(): pl.pallas_call(functools.partial(kernel, groups, ranks), out_shape=jax.Sh...  9.2 us
    unnamed x1, local copies, waits for them, and re-layouts  1.54 us

profile of v2, /device:TPU:0, one launch (start us, length us, event | category | flops | bytes accessed | tf_op | source)
XLA Modules:
  0.0 10.7 jit_solution(4497991061536187844)
XLA Ops:
  0.0 9.2 %shard_map.82 = f32[6,8,512]{2,1,0:T(8,128)} custom-call(f32[6,8,512]{2,1,0:T(8,128)} %bitcast.3, s32[1,4,96]{2,1,0:T(4,128)} %map_hbm.1, s32[8]{0:T(128)} %material_hbm.1, f32[4,64,64]{2,1,0:T(8,128)} %proj_hbm.1, s32[8,6]{1,0:T(8,128)} %nb_hbm.1, s32[1,6]{1,0:T(1,128)} %count_hbm.1, f32[8]{0:T(128)} %metric_hbm.1, bf16[256,256]{1,0:T(8,128)(2,1)} %constant.2.clone.deriv_hbm), custom_call_target="tpu_custom_call" | custom-call | tf_op jit(solution)/shard_map/pallas_call | solution.py:509
  9.2 1.5 %copy.10 = f32[8,6,512]{2,0,1:T(8,128)} copy(f32[8,6,512]{2,0,1:T(8,128)} %bitcast.2) | data formatting | bytes 196608

commit v3 on v2

--- a/solution.py
+++ b/solution.py
@@ -508,7 +508,7 @@
     in_smem = (2, 5, 6)
     result = pl.pallas_call(
         functools.partial(kernel, groups, ranks),
-        out_shape=jax.ShapeDtypeStruct(by_variable.shape, state.dtype),
+        out_shape=pltpu.VMEM(by_variable.shape, state.dtype),
         in_specs=[pl.BlockSpec(memory_space=pltpu.HBM)] * len(operands),
         out_specs=pl.BlockSpec(memory_space=pltpu.VMEM),
         scratch_shapes=[
@@ -523,9 +523,9 @@
             pltpu.SemaphoreType.DMA((len(operands),)),
         ],
         compiler_params=pltpu.CompilerParams(
-            collective_id=0, has_side_effects=True, vmem_limit_bytes=56 * 2**20
+            collective_id=0, has_side_effects=True, vmem_limit_bytes=40 * 2**20
         ),
-    )(*operands)
+    )(*[pltpu.with_memory_space_constraint(x, pltpu.HBM) for x in operands])
     return jnp.transpose(result, (1, 0, 2))
 
 

time: 10.9 us -> 9.37 us (0.86)
  local copies, waits for them, and re-layouts: 1.54 us -> 0.64 us
  Pallas kernels: 9.2 us -> 8.57 us
    unnamed x1, local copies, waits for them, and re-layouts: 1.54 us -> 0.64 us
    pallas_call x1, Pallas kernels: 9.2 us -> 8.57 us  [shards(): pl.pallas_call(functools.partial(kernel, groups, ranks), out_shape=pltpu....]
where the time goes in v3:
time: 9.37 us; the launch traced here: 9.23 us
  Pallas kernels  8.57 us (91%)
  local copies, waits for them, and re-layouts  0.64 us (7%)
    pallas_call x1, Pallas kernels, shards(): pl.pallas_call(functools.partial(kernel, groups, ranks), out_shape=pltpu....  8.57 us
    unnamed x1, local copies, waits for them, and re-layouts  0.64 us

profile of v3, /device:TPU:0, one launch (start us, length us, event | category | flops | bytes accessed | tf_op | source)
XLA Modules:
  0.0 9.2 jit_solution(11279269603685215129)
XLA Ops:
  0.0 8.6 %shard_map.82 = f32[6,8,512]{2,1,0:T(8,128)S(1)} custom-call(f32[6,8,512]{2,1,0:T(8,128)} %bitcast.3, s32[1,4,96]{2,1,0:T(4,128)} %map_hbm.1, s32[8]{0:T(128)} %material_hbm.1, f32[4,64,64]{2,1,0:T(8,128)} %proj_hbm.1, s32[8,6]{1,0:T(8,128)} %nb_hbm.1, s32[1,6]{1,0:T(1,128)} %count_hbm.1, f32[8]{0:T(128)} %metric_hbm.1, bf16[256,256]{1,0:T(8,128)(2,1)} %constant.2.clone.deriv_hbm), custom_call_target="tpu_custom_call" | custom-call | tf_op jit(solution)/shard_map/pallas_call | solution.py:509
  8.6 0.6 %copy.10 = f32[8,6,512]{2,0,1:T(8,128)} copy(f32[8,6,512]{2,0,1:T(8,128)S(1)} %bitcast.2) | data formatting | bytes 196608

commit v4 on v3

--- a/solution.py
+++ b/solution.py
@@ -73,8 +73,8 @@
     return speed, pressure, jnp.sqrt(heat * pressure * inverse)
 
 
-def flux_jump(own, other, own_heat, other_heat, normal):
-    s_l, p_l, c_l = side(own, own_heat, normal)
+def flux_jump(own, other, own_side, other_heat, normal):
+    s_l, p_l, c_l = own_side
     s_r, p_r, c_r = side(other, other_heat, normal)
     wave_l = jnp.minimum(s_l - c_l, s_r - c_r)
     wave_r = jnp.maximum(s_l + c_l, s_r + c_r)
@@ -141,8 +141,8 @@
 def kernel(
     groups,
     ranks,
+    map_hbm,
     state_hbm,
-    map_hbm,
     material_hbm,
     proj_hbm,
     nb_hbm,
@@ -150,8 +150,8 @@
     metric_hbm,
     deriv_hbm,
     out_ref,
+    map_ref,
     state_ref,
-    map_ref,
     material_ref,
     proj_ref,
     nb_ref,
@@ -168,8 +168,8 @@
         pltpu.make_async_copy(src, dst, fetch_sem.at[i])
         for i, (src, dst) in enumerate(
             (
+                (map_hbm, map_ref),
                 (state_hbm, state_ref),
-                (map_hbm, map_ref),
                 (material_hbm, material_ref),
                 (proj_hbm, proj_ref),
                 (nb_hbm, nb_ref),
@@ -179,7 +179,7 @@
             )
         )
     ]
-    for fetch in fetches:
+    for fetch in fetches[:4]:
         fetch.start()
     elem = lax.axis_index("elem")
     grp = lax.axis_index("grp")
@@ -199,6 +199,8 @@
     def _():
         pl.semaphore_signal(barrier, inc=1, device_id=(elem - 1, grp), device_id_type=MESH)
 
+    for fetch in fetches[4:]:
+        fetch.start()
     slots = map_ref.shape[2]
     elems = state_ref.shape[1]
     nodes = state_ref.shape[2]
@@ -218,7 +220,22 @@
     second = jnp.where((code & 2) != 0, 7 - second, second)
     turn = jnp.where((iota((LANES, 512), 0) & 63) == 8 * first + second, 1.0, 0.0).astype(bf16)
     same = iota((slots, slots), 0) == iota((slots, slots), 1)
-    for fetch in fetches[:3]:
+    fetches[0].wait()
+    info = map_ref[0].astype(f32)
+    spread = mm(
+        jnp.concatenate([jnp.where(same, info[i : i + 1], 0.0) for i in range(4)], axis=0),
+        jnp.ones((slots, LANES), f32),
+    ).astype(jnp.int32)
+    owner, face, sub, orient = [spread[i * slots : (i + 1) * slots] for i in range(4)]
+    half = jnp.where(iota((slots, LANES), 1) >= FN, 1, 0)
+    upper = half == 1
+    dim, end = face >> 1, face & 1
+    at_end = end == half
+    rows = 3 * elems
+    place = dim * elems + owner
+    one_hot = jnp.where(place[:, : 2 * rows] == (iota((slots, 2 * rows), 1) % rows), 1.0, 0.0).astype(bf16)
+
+    for fetch in fetches[1:3]:
         fetch.wait()
     u = [state_ref[v] for v in range(NV)]
     heats = [1.4 + 0.27 * material_ref[j].astype(f32) for j in range(elems)]
@@ -236,26 +253,12 @@
             ]
         )
 
-    info = map_ref[0].astype(f32)
-    spread = mm(
-        jnp.concatenate([jnp.where(same, info[i : i + 1], 0.0) for i in range(4)], axis=0),
-        jnp.ones((slots, LANES), f32),
-    ).astype(jnp.int32)
-    owner, face, sub, orient = [spread[i * slots : (i + 1) * slots] for i in range(4)]
-    half = jnp.where(iota((slots, LANES), 1) >= FN, 1, 0)
-    upper = half == 1
-    dim, end = face >> 1, face & 1
-
     high, low = split(
         jnp.concatenate(
             [jnp.concatenate([trace[v][d] for v in range(NV)], axis=1) for d in range(3)], axis=0
         )
     )
-    rows = 3 * elems
-    place = dim * elems + owner
-    one_hot = jnp.where(place[:, : 2 * rows] == (iota((slots, 2 * rows), 1) % rows), 1.0, 0.0)
     picked = mm(one_hot, jnp.concatenate([high, low], axis=0))
-    at_end = end == half
     parts = [
         jnp.where(at_end, picked[:, v * LANES : (v + 1) * LANES], 0.0) for v in range(NV)
     ]
@@ -355,7 +358,7 @@
             other_heat = jnp.where(here, heats[j], other_heat)
         normal = [None, None, None]
         normal[d] = sign
-        jump = flux_jump(own, other, heat, other_heat, normal)
+        jump = flux_jump(own, other, side(own, heat, normal), other_heat, normal)
         local.append([jnp.where(across >= 0, x, 0.0) for x in jump])
 
     heat_all = jnp.concatenate([heat] * chunks, axis=1)
@@ -423,6 +426,17 @@
     gather_at = (map_ref[0, 1:2, :] >> 1) * elems + map_ref[0, 0:1, :]
     gather = jnp.where(iota((3 * elems, slots), 0) == gather_at, 1.0, 0.0).astype(bf16)
 
+    native_side = side(native, native_heat, normal)
+    scale = jnp.full((TILE, LANES), metric_ref[0], f32)
+    for j in range(1, elems):
+        scale = jnp.where(row8 == j, metric_ref[j], scale)
+    scale = step_size * scale
+    base = [
+        [u[v][:, j * LANES : (j + 1) * LANES] + scale * volume[v][j] for j in range(chunks)]
+        for v in range(NV)
+    ]
+    scale = lift_weight * scale
+
     for off in range(1, groups):
         from_peer(off).wait_recv()
 
@@ -441,7 +455,7 @@
         partner += [jnp.where(upper, moved, plane), jnp.where(upper, plane, moved)]
     partner = [jnp.where(live, a, b) for a, b in zip(partner, native)]
     partner_heat = jnp.where(live, recv[:, 3].reshape(slots, LANES), native_heat)
-    jump = flux_jump(native, partner, native_heat, partner_heat, normal)
+    jump = flux_jump(native, partner, native_side, partner_heat, normal)
     corr = [jnp.where(live, back_weight * x, 0.0) for x in jump]
 
     parts = chosen_quad(mm(split_columns(corr, upper), quads_back), corr, sub, half)
@@ -465,10 +479,6 @@
     high, low = split(wide)
     both = mm_t(jnp.concatenate([high, low], axis=0), pick_nodes)
     surface = both[: NV * elems] + both[NV * elems :]
-    scale = jnp.full((TILE, LANES), metric_ref[0], f32)
-    for j in range(1, elems):
-        scale = jnp.where(row8 == j, metric_ref[j], scale)
-    scale = step_size * scale
     for v in range(NV):
         for j in range(chunks):
             s = surface[v * elems : (v + 1) * elems, j * LANES : (j + 1) * LANES]
@@ -477,7 +487,7 @@
             if j == chunks - 1:
                 s = s + jnp.where(upper8, lines[v][0], 0.0)
             at = slice(j * LANES, (j + 1) * LANES)
-            out_ref[v, :, at] = u[v][:, at] + scale * (volume[v][j] + lift_weight * s)
+            out_ref[v, :, at] = base[v][j] + scale * s
 
     for off in range(1, groups):
         to_peer(off).wait_send()
@@ -496,8 +506,8 @@
     blocks = mortar_map.shape[2] // TILE
     by_variable = jnp.transpose(state, (1, 0, 2))
     operands = (
+        mortar_map,
         by_variable,
-        mortar_map,
         material,
         mortar_proj,
         neighbours,

time: 9.37 us -> 9.36 us (level)
  no operation moved by 1% of the time
where the time goes in v4:
time: 9.36 us; the launch traced here: 9.2 us
  Pallas kernels  8.55 us (91%)
  local copies, waits for them, and re-layouts  0.64 us (7%)
    pallas_call x1, Pallas kernels, shards(): pl.pallas_call(functools.partial(kernel, groups, ranks), out_shape=pltpu....  8.55 us
    unnamed x1, local copies, waits for them, and re-layouts  0.64 us

profile of v4, /device:TPU:0, one launch (start us, length us, event | category | flops | bytes accessed | tf_op | source)
XLA Modules:
  0.0 9.2 jit_solution(6096639277963187244)
XLA Ops:
  0.0 8.6 %shard_map.82 = f32[6,8,512]{2,1,0:T(8,128)S(1)} custom-call(s32[1,4,96]{2,1,0:T(4,128)} %map_hbm.1, f32[6,8,512]{2,1,0:T(8,128)} %bitcast.3, s32[8]{0:T(128)} %material_hbm.1, f32[4,64,64]{2,1,0:T(8,128)} %proj_hbm.1, s32[8,6]{1,0:T(8,128)} %nb_hbm.1, s32[1,6]{1,0:T(1,128)} %count_hbm.1, f32[8]{0:T(128)} %metric_hbm.1, bf16[256,256]{1,0:T(8,128)(2,1)} %constant.2.clone.deriv_hbm), custom_call_target="tpu_custom_call" | custom-call | tf_op jit(solution)/shard_map/pallas_call | solution.py:519
  8.6 0.6 %copy.10 = f32[8,6,512]{2,0,1:T(8,128)} copy(f32[8,6,512]{2,0,1:T(8,128)S(1)} %bitcast.2) | data formatting | bytes 196608

commit v5 on v4

--- a/solution.py
+++ b/solution.py
@@ -258,33 +258,36 @@
             [jnp.concatenate([trace[v][d] for v in range(NV)], axis=1) for d in range(3)], axis=0
         )
     )
-    picked = mm(one_hot, jnp.concatenate([high, low], axis=0))
-    parts = [
-        jnp.where(at_end, picked[:, v * LANES : (v + 1) * LANES], 0.0) for v in range(NV)
-    ]
-
-    high, low = split(jnp.concatenate(parts, axis=0))
-    turned = mm(
-        jnp.concatenate([high, low], axis=1), jnp.concatenate([turn, turn], axis=0)
-    )
-    parts = chosen_turn(turned, orient, half)
-
+    by_place = jnp.concatenate([high, low], axis=0).astype(bf16)
+    turn_twice = jnp.concatenate([turn, turn], axis=0)
     fetches[3].wait()
     quads = proj_ref[...].reshape(4 * FN, FN)
     quad_high, quad_low = split(quads)
-    projected = mm_t(
-        split_columns(parts, upper),
-        jnp.concatenate([quad_high, quad_high, quad_low, jnp.zeros_like(quad_low)], axis=1),
-    )
-    native = chosen_quad(projected, parts, sub, half)
+    quads_out = jnp.concatenate(
+        [quad_high, quad_high, quad_low, jnp.zeros_like(quad_low)], axis=1
+    ).astype(bf16)
+
+    def mortar_traces(at):
+        picked = mm(one_hot[at], by_place)
+        parts = [
+            jnp.where(at_end[at], picked[:, v * LANES : (v + 1) * LANES], 0.0) for v in range(NV)
+        ]
+        high, low = split(jnp.concatenate(parts, axis=0))
+        turned = mm(jnp.concatenate([high, low], axis=1), turn_twice)
+        parts = chosen_turn(turned, orient[at], half[at])
+        projected = mm_t(split_columns(parts, upper[at]), quads_out)
+        parts = chosen_quad(projected, parts, sub[at], half[at])
+        tiles = slice(at.start // TILE, at.stop // TILE)
+        for i in range(3):
+            plane = jnp.where(upper[at], parts[2 * i + 1], parts[2 * i])
+            send[tiles, i] = plane.reshape(-1, TILE, LANES)
+        send[tiles, 3] = native_heat[at].reshape(-1, TILE, LANES)
+        return parts
+
     native_heat = jnp.full((slots, LANES), heats[0], f32)
     for j in range(1, elems):
         native_heat = jnp.where(owner == j, heats[j], native_heat)
 
-    for i in range(3):
-        plane = jnp.where(upper, native[2 * i + 1], native[2 * i])
-        send[:, i] = plane.reshape(blocks, TILE, LANES)
-    send[:, 3] = native_heat.reshape(blocks, TILE, LANES)
     many = CAPS // TILE
     up_at, down_at = pl.ds(groups, many), pl.ds(groups + many, many)
 
@@ -321,6 +324,7 @@
         )
 
     up_sem, down_sem = groups, groups + 1
+    elem_native = mortar_traces(slice(groups * CAPG, slots))
     pl.semaphore_wait(
         barrier, groups - 1 + has_up.astype(jnp.int32) + has_down.astype(jnp.int32)
     )
@@ -333,8 +337,10 @@
     def _():
         along(down_at, up_at, down_sem, -1).start()
 
+    grp_native = mortar_traces(slice(0, groups * CAPG))
     for off in range(1, groups):
         to_peer(off).start()
+    native = [jnp.concatenate(x, axis=0) for x in zip(grp_native, elem_native)]
 
     for fetch in fetches[4:]:
         fetch.wait()

time: 9.36 us -> 9.38 us (level)
  no operation moved by 1% of the time
where the time goes in v5:
time: 9.38 us; the launch traced here: 9.23 us
  Pallas kernels  8.58 us (91%)
  local copies, waits for them, and re-layouts  0.64 us (7%)
    pallas_call x1, Pallas kernels, shards(): pl.pallas_call(functools.partial(kernel, groups, ranks), out_shape=pltpu....  8.58 us
    unnamed x1, local copies, waits for them, and re-layouts  0.64 us

profile of v5, /device:TPU:0, one launch (start us, length us, event | category | flops | bytes accessed | tf_op | source)
XLA Modules:
  0.0 9.2 jit_solution(1817384588364669860)
XLA Ops:
  0.0 8.6 %shard_map.82 = f32[6,8,512]{2,1,0:T(8,128)S(1)} custom-call(s32[1,4,96]{2,1,0:T(4,128)} %map_hbm.1, f32[6,8,512]{2,1,0:T(8,128)} %bitcast.3, s32[8]{0:T(128)} %material_hbm.1, f32[4,64,64]{2,1,0:T(8,128)} %proj_hbm.1, s32[8,6]{1,0:T(8,128)} %nb_hbm.1, s32[1,6]{1,0:T(1,128)} %count_hbm.1, f32[8]{0:T(128)} %metric_hbm.1, bf16[256,256]{1,0:T(8,128)(2,1)} %constant.2.clone.deriv_hbm), custom_call_target="tpu_custom_call" | custom-call | tf_op jit(solution)/shard_map/pallas_call | solution.py:525
  8.6 0.6 %copy.10 = f32[8,6,512]{2,0,1:T(8,128)} copy(f32[8,6,512]{2,0,1:T(8,128)S(1)} %bitcast.2) | data formatting | bytes 196608
